TPU v7x, 512 devices: a whole 4x4x16 slice. The times are simulated.
512 devices in a mesh: dp: 4 (over y), tm: 8 (over x, core), tile: 16 (over z).
Axes of the slice: x: 4, y: 4, z: 16, core: 2. Of those that a mesh axis runs over, the one named last changes fastest.
Arguments:
- frames_in: bfloat16 [4, 8, 48, 512, 128], P('dp', 'tm', None, 'tile'), may hold values from -6 to 6
- w_in: bfloat16 [96, 432], replicated, may hold values from -0.3125 to 0.3125
- gate_bias: float32 [48], replicated, may hold values from -1 to 3
- w_ent: bfloat16 [96, 864], replicated, may hold values from -0.21875 to 0.21875
- active_tiles: int32 [4, 8, 16, 12], P('dp', 'tm', 'tile'), may hold values from 0 to 15, as said below
- active_count: int32 [4, 8, 16], P('dp', 'tm', 'tile'), may hold values from 1 to 12, as said below
- cotangent: bfloat16 [4, 8, 16, 12, 48, 256], P('dp', 'tm', 'tile'), may hold values from -6 to 6
Outputs:
- latent: bfloat16 [4, 8, 16, 12, 48, 256], P('dp', 'tm', 'tile')
- weight_grad: float32 [96, 864], P('dp')
Inputs may be any that keep to these rules, and one draw needn't show every extreme that they name: `active_tiles`: the entries of one band's list are different tile numbers; only the first active_count of them are used. `active_count`: in every clip and frame some band has 12 active tiles.
All inputs are finite; a program needn't handle non-finite values.
Results may differ from a plain program's by a relative error of at most 0.0038.
Values may be sent and summed in bfloat16 or wider, within the bound.
A program may use at most 64 MiB of HBM per device.

v0:
```python
import jax
import jax.numpy as jnp
from jax import lax
from jax.sharding import PartitionSpec as P


def extended(value, sides, width):
    for axis, dim in sides:
        size, length = (lax.axis_size(axis), value.shape[dim])
        up = [(i, (i + 1) % size) for i in range(size - 1)]
        down = [(j, i) for i, j in up]
        last = lax.slice_in_dim(value, length - width, length, axis=dim)
        initial = lax.slice_in_dim(value, 0, width, axis=dim)
        before = lax.ppermute(last, axis, up)
        after = lax.ppermute(initial, axis, down)
        value = jnp.concatenate([before, value, after], axis=dim)
    return value


def shifted(block, axis, distance):
    devices = range(lax.axis_size(axis))
    route = [(i - distance, i) for i in devices if i - distance in devices]
    return lax.ppermute(block, axis, route)


def tile_patches(block):
    chans2 = block.shape[0]
    stacked = jnp.stack(
        [block[:, dy : dy + 16, dx : dx + 16] for dy in range(3) for dx in range(3)]
    )
    return stacked.reshape(9 * chans2, 256)


def entropy_terms(pre, target, cot, chans):
    mean = pre[:chans]
    spread = pre[chans:]
    sigma = 0.5 + jax.nn.softplus(spread)
    lat = (target - mean) / sigma
    push = jnp.concatenate([-cot / sigma, -cot * lat * jax.nn.sigmoid(spread) / sigma], axis=0)
    return (lat, push)


def body(frames_in, w_in, gate_bias, w_ent, active_tiles, active_count, cotangent):
    frame = frames_in[0, 0]
    chans, rows, cols = frame.shape
    edged = extended(frame, (("tile", 1),), 1)
    padded = jnp.pad(edged, ((0, 0), (0, 0), (1, 1)))
    stacked = jnp.stack(
        [padded[:, dy : dy + rows, dx : dx + cols] for dy in range(3) for dx in range(3)]
    )
    mixed = jnp.dot(
        w_in, stacked.reshape(9 * chans, rows * cols), preferred_element_type=jnp.float32
    )
    gate = jax.nn.sigmoid(mixed[:chans] + gate_bias[:, None])
    drive = jnp.tanh(mixed[chans:])

    def relay(step, state):
        return shifted(gate * state + drive, "tm", 1)

    context = lax.fori_loop(0, lax.axis_size("tm") - 1, relay, jnp.zeros_like(drive))
    context_bf = context.astype(jnp.bfloat16).reshape(chans, rows, cols)
    context_rim = extended(context_bf, (("tile", 1),), 1)
    joined = jnp.pad(jnp.concatenate([edged, context_rim], axis=0), ((0, 0), (0, 0), (1, 1)))
    tile_list = active_tiles[0, 0, 0]
    count = active_count[0, 0, 0]
    cot_slots = cotangent[0, 0, 0]
    kslots = tile_list.shape[0]
    across = cols // 16

    def one_tile(slot, carry):
        latents, grad = carry
        ident = tile_list[slot]
        row0 = 16 * (ident // across)
        col0 = 16 * (ident % across)
        block = lax.dynamic_slice(joined, (0, row0, col0), (2 * chans, 18, 18))
        patches = tile_patches(block)
        pre = jnp.dot(w_ent, patches, preferred_element_type=jnp.float32)
        target = (
            lax.dynamic_slice(frame, (0, row0, col0), (chans, 16, 16))
            .reshape(chans, 256)
            .astype(jnp.float32)
        )
        lat, push = entropy_terms(pre, target, cot_slots[slot].astype(jnp.float32), chans)
        grad = grad + jnp.dot(
            push.astype(jnp.bfloat16), patches.T, preferred_element_type=jnp.float32
        )
        latents = lax.dynamic_update_slice(latents, lat.astype(jnp.bfloat16)[None], (slot, 0, 0))
        return (latents, grad)

    start = (
        jnp.zeros((kslots, chans, 256), jnp.bfloat16),
        jnp.zeros((2 * chans, 18 * chans), jnp.float32),
    )
    latents, grad = lax.fori_loop(0, count, one_tile, start)
    total = lax.psum(grad, ("tm", "tile"))
    share = lax.psum_scatter(total, "dp", scatter_dimension=0, tiled=True)
    return (latents[None, None, None], share)


def solution(mesh):
    return jax.shard_map(
        body,
        mesh=mesh,
        in_specs=(
            P("dp", "tm", None, "tile", None),
            P(),
            P(),
            P(),
            P("dp", "tm", "tile", None),
            P("dp", "tm", "tile"),
            P("dp", "tm", "tile", None, None, None),
        ),
        out_specs=(P("dp", "tm", "tile", None, None, None), P("dp", None)),
        check_vma=False,
    )
```

profile of v0, /device:TPU:1, one launch (start us, length us, event | category | flops | bytes accessed | tf_op | source)
XLA Modules:
  0.0 587.8 jit_solution(12114362477629338827)
XLA Ops:
  7.2 1.2 copy.69
  8.4 4.4 collective-permute-start.1
  12.8 1.3 collective-permute-start.2
  14.1 3.3 collective-permute-done.2
  20.1 1.4 convolution_bitcast_fusion.1
  21.9 94.5 %while.24 = (s32[]{:T(128)}, f32[48,4096]{1,0:T(8,128)S(1)}, f32[48,4096]{1,0:T(8,128)S(1)}, f32[48,4096]{1,0:T(8,128)S(1)}, s32[]{:T(128)}) while((s32[]{:T(128)}, f32[48,4096]{1,0:T(8,128)S(1)}, f32[48,4096]{1,0:T(8,128)S(1)}, f32[48,4096]{1,0:T(8,128)S(1)}, s32[]{:T(128)}) %tuple.58), condition=%wide.region_1.2_spmd, body=%wide.region_0.1_spmd.sunk | while | flops 393218 | bytes 6291557 | solution.py:60
  22.0 4.9 collective-permute-start
  26.9 8.9 %collective-permute-done = f32[48,4096]{1,0:T(8,128)S(1)} collective-permute-done((f32[48,4096]{1,0:T(8,128)S(1)}, f32[48,4096]{1,0:T(8,128)S(1)}, u32[]{:S(2)}, u32[]{:S(2)}) %collective-permute-start) | collective-permute-done | bytes 786464 | tf_op jit(solution)/shard_map/while/body/eval_jaxpr/ppermute | solution.py:23
  35.9 4.4 collective-permute-start
  40.3 8.9 %collective-permute-done = f32[48,4096]{1,0:T(8,128)S(1)} collective-permute-done((f32[48,4096]{1,0:T(8,128)S(1)}, f32[48,4096]{1,0:T(8,128)S(1)}, u32[]{:S(2)}, u32[]{:S(2)}) %collective-permute-start) | collective-permute-done | bytes 786464 | tf_op jit(solution)/shard_map/while/body/eval_jaxpr/ppermute | solution.py:23
  49.4 4.4 collective-permute-start
  53.8 8.9 %collective-permute-done = f32[48,4096]{1,0:T(8,128)S(1)} collective-permute-done((f32[48,4096]{1,0:T(8,128)S(1)}, f32[48,4096]{1,0:T(8,128)S(1)}, u32[]{:S(2)}, u32[]{:S(2)}) %collective-permute-start) | collective-permute-done | bytes 786464 | tf_op jit(solution)/shard_map/while/body/eval_jaxpr/ppermute | solution.py:23
  62.8 4.4 collective-permute-start
  67.2 8.9 %collective-permute-done = f32[48,4096]{1,0:T(8,128)S(1)} collective-permute-done((f32[48,4096]{1,0:T(8,128)S(1)}, f32[48,4096]{1,0:T(8,128)S(1)}, u32[]{:S(2)}, u32[]{:S(2)}) %collective-permute-start) | collective-permute-done | bytes 786464 | tf_op jit(solution)/shard_map/while/body/eval_jaxpr/ppermute | solution.py:23
  76.2 4.4 collective-permute-start
  80.6 8.9 %collective-permute-done = f32[48,4096]{1,0:T(8,128)S(1)} collective-permute-done((f32[48,4096]{1,0:T(8,128)S(1)}, f32[48,4096]{1,0:T(8,128)S(1)}, u32[]{:S(2)}, u32[]{:S(2)}) %collective-permute-start) | collective-permute-done | bytes 786464 | tf_op jit(solution)/shard_map/while/body/eval_jaxpr/ppermute | solution.py:23
  89.7 4.4 collective-permute-start
  94.1 8.9 %collective-permute-done = f32[48,4096]{1,0:T(8,128)S(1)} collective-permute-done((f32[48,4096]{1,0:T(8,128)S(1)}, f32[48,4096]{1,0:T(8,128)S(1)}, u32[]{:S(2)}, u32[]{:S(2)}) %collective-permute-start) | collective-permute-done | bytes 786464 | tf_op jit(solution)/shard_map/while/body/eval_jaxpr/ppermute | solution.py:23
  103.1 4.4 collective-permute-start
  107.5 8.9 %collective-permute-done = f32[48,4096]{1,0:T(8,128)S(1)} collective-permute-done((f32[48,4096]{1,0:T(8,128)S(1)}, f32[48,4096]{1,0:T(8,128)S(1)}, u32[]{:S(2)}, u32[]{:S(2)}) %collective-permute-start) | collective-permute-done | bytes 786464 | tf_op jit(solution)/shard_map/while/body/eval_jaxpr/ppermute | solution.py:23
  116.6 3.5 collective-permute-start.3
  120.2 1.3 collective-permute-start.4
  121.5 1.5 copy.47
  123.1 2.9 collective-permute-done.4
  126.1 0.7 copy.50
  127.3 0.7 broadcast_in_dim.19
  128.0 93.2 %while.25 = (s32[]{:T(128)}, bf16[12,48,256]{2,1,0:T(8,128)(2,1)}, f32[96,864]{1,0:T(8,128)S(1)}, s32[]{:T(128)}, s32[12]{0:T(128)S(1)}, /*index=5*/bf16[48,32,1...) while((s32[]{:T(128)}, bf16[12,48,256]{2,1,0:T(8,128)(2,1)}, ...), condition=%wide.region_3.4_spmd, body=%wide.region_2.3_spmd.sunk | while | flops 85496864 | bytes 5409484 | solution.py:94
  132.8 0.7 reshape.31
  133.8 0.9 constant_dynamic-slice_fusion.2
  134.7 0.8 fusion.66
  141.2 0.7 reshape.31
  142.2 0.9 constant_dynamic-slice_fusion.2
  143.1 0.8 fusion.66
  149.6 0.7 reshape.31
  150.6 0.9 constant_dynamic-slice_fusion.2
  151.5 0.8 fusion.66
  158.0 0.7 reshape.31
  159.0 0.9 constant_dynamic-slice_fusion.2
  159.9 0.8 fusion.66
  166.4 0.7 reshape.31
  167.4 0.9 constant_dynamic-slice_fusion.2
  168.4 0.8 fusion.66
  174.8 0.7 reshape.31
  175.8 0.9 constant_dynamic-slice_fusion.2
  176.8 0.8 fusion.66
  183.2 0.7 reshape.31
  184.2 0.9 constant_dynamic-slice_fusion.2
  185.2 0.8 fusion.66
  191.6 0.7 reshape.31
  192.6 0.9 constant_dynamic-slice_fusion.2
  193.6 0.8 fusion.66
  200.0 0.7 reshape.31
  201.0 0.9 constant_dynamic-slice_fusion.2
  202.0 0.8 fusion.66
  208.5 0.7 reshape.31
  209.5 0.9 constant_dynamic-slice_fusion.2
  210.4 0.8 fusion.66
  216.9 0.7 reshape.31
  217.9 0.9 constant_dynamic-slice_fusion.2
  218.8 0.8 fusion.66
  221.2 0.7 copy-done.1
  222.0 38.5 %reduce-scatter.4.cloned.1.call-done = f32[24,864]{1,0:T(8,128)} async-done(((f32[96,864]{1,0:T(8,128)}), f32[24,864]{1,0:T(8,128)}) %reduce-scatter.4.cloned.1.call-update) | async-done | bytes 82960
  260.5 318.9 %all-reduce.5.cloned.1.call-done = f32[24,864]{1,0:T(8,128)} async-done(((f32[24,864]{1,0:T(8,128)}), f32[24,864]{1,0:T(8,128)}) %all-reduce.5.cloned.1.call-update) | async-done | bytes 82960 | tf_op jit(solution)/shard_map/psum | solution.py:95
  579.4 1.5 copy.107
  (230 shorter events, 34.5 us)
Async XLA Ops:
  7.2 12.9 %copy-start = (bf16[96,432]{1,0:T(8,128)(2,1)S(1)}, bf16[96,432]{1,0:T(8,128)(2,1)}, u32[]{:S(2)}) copy-start(bf16[96,432]{1,0:T(8,128)(2,1)} %param.12) | copy-start | bytes 248836
  7.2 253.3 %reduce-scatter.4.cloned.1.call-start = ((), (), s32[]{:S(2)}) async-start(), calls=%async_computation.2 | async-start | bytes 430080
  8.4 10.1 %copy-start.2 = (bf16[1,1,48,32,128]{4,2,3,1,0:T(8,128)(2,1)}, bf16[1,1,48,32,128]{4,2,3,1,0:T(8,128)(2,1)S(1)}, u32[]{:S(2)}) copy-start(bf16[1,1,48,32,128]{4,2,3,1,0:T(8,128)(2,1)S(1)} %copy.69) | copy-start | bytes 1179652
  8.4 5.7 collective-permute-start.1
  12.8 4.6 collective-permute-start.2
  18.4 1.0 copy-start.5
  20.1 1.4 copy-start.7
  22.0 13.8 %collective-permute-start = (f32[48,4096]{1,0:T(8,128)S(1)}, f32[48,4096]{1,0:T(8,128)S(1)}, u32[]{:S(2)}, u32[]{:S(2)}) collective-permute-start(f32[48,4096]{1,0:T(8,128)S(1)} %multiply_add_fusion.2), channel_id=1, source_target_pairs={{0,16},{16,32},{32,48},{48,64},{64,80},{80,96},{96,112},{1,17},{17... | collective-permute-start | bytes 2359304 | tf_op jit(solution)/shard_map/while/body/eval_jaxpr/ppermute | solution.py:23
  35.9 13.3 %collective-permute-start = (f32[48,4096]{1,0:T(8,128)S(1)}, f32[48,4096]{1,0:T(8,128)S(1)}, u32[]{:S(2)}, u32[]{:S(2)}) collective-permute-start(f32[48,4096]{1,0:T(8,128)S(1)} %multiply_add_fusion.2), channel_id=1, source_target_pairs={{0,16},{16,32},{32,48},{48,64},{64,80},{80,96},{96,112},{1,17},{17... | collective-permute-start | bytes 2359304 | tf_op jit(solution)/shard_map/while/body/eval_jaxpr/ppermute | solution.py:23
  49.4 13.3 %collective-permute-start = (f32[48,4096]{1,0:T(8,128)S(1)}, f32[48,4096]{1,0:T(8,128)S(1)}, u32[]{:S(2)}, u32[]{:S(2)}) collective-permute-start(f32[48,4096]{1,0:T(8,128)S(1)} %multiply_add_fusion.2), channel_id=1, source_target_pairs={{0,16},{16,32},{32,48},{48,64},{64,80},{80,96},{96,112},{1,17},{17... | collective-permute-start | bytes 2359304 | tf_op jit(solution)/shard_map/while/body/eval_jaxpr/ppermute | solution.py:23
  62.8 13.3 %collective-permute-start = (f32[48,4096]{1,0:T(8,128)S(1)}, f32[48,4096]{1,0:T(8,128)S(1)}, u32[]{:S(2)}, u32[]{:S(2)}) collective-permute-start(f32[48,4096]{1,0:T(8,128)S(1)} %multiply_add_fusion.2), channel_id=1, source_target_pairs={{0,16},{16,32},{32,48},{48,64},{64,80},{80,96},{96,112},{1,17},{17... | collective-permute-start | bytes 2359304 | tf_op jit(solution)/shard_map/while/body/eval_jaxpr/ppermute | solution.py:23
  76.2 13.3 %collective-permute-start = (f32[48,4096]{1,0:T(8,128)S(1)}, f32[48,4096]{1,0:T(8,128)S(1)}, u32[]{:S(2)}, u32[]{:S(2)}) collective-permute-start(f32[48,4096]{1,0:T(8,128)S(1)} %multiply_add_fusion.2), channel_id=1, source_target_pairs={{0,16},{16,32},{32,48},{48,64},{64,80},{80,96},{96,112},{1,17},{17... | collective-permute-start | bytes 2359304 | tf_op jit(solution)/shard_map/while/body/eval_jaxpr/ppermute | solution.py:23
  89.7 13.3 %collective-permute-start = (f32[48,4096]{1,0:T(8,128)S(1)}, f32[48,4096]{1,0:T(8,128)S(1)}, u32[]{:S(2)}, u32[]{:S(2)}) collective-permute-start(f32[48,4096]{1,0:T(8,128)S(1)} %multiply_add_fusion.2), channel_id=1, source_target_pairs={{0,16},{16,32},{32,48},{48,64},{64,80},{80,96},{96,112},{1,17},{17... | collective-permute-start | bytes 2359304 | tf_op jit(solution)/shard_map/while/body/eval_jaxpr/ppermute | solution.py:23
  103.1 13.3 %collective-permute-start = (f32[48,4096]{1,0:T(8,128)S(1)}, f32[48,4096]{1,0:T(8,128)S(1)}, u32[]{:S(2)}, u32[]{:S(2)}) collective-permute-start(f32[48,4096]{1,0:T(8,128)S(1)} %multiply_add_fusion.2), channel_id=1, source_target_pairs={{0,16},{16,32},{32,48},{48,64},{64,80},{80,96},{96,112},{1,17},{17... | collective-permute-start | bytes 2359304 | tf_op jit(solution)/shard_map/while/body/eval_jaxpr/ppermute | solution.py:23
  116.4 5.1 copy-start.6
  116.5 9.6 %copy-start.3 = (bf16[1,1,48,32,128]{4,2,3,1,0:T(8,128)(2,1)S(1)}, bf16[1,1,48,32,128]{4,2,3,1,0:T(8,128)(2,1)}, u32[]{:S(2)}) copy-start(bf16[1,1,48,32,128]{4,2,3,1,0:T(8,128)(2,1)} %copy-done.2) | copy-start | bytes 1179652
  116.6 6.5 %collective-permute-start.3 = (bf16[48,1,128]{2,1,0:T(2,128)(2,1)S(1)}, bf16[48,1,128]{2,1,0:T(2,128)(2,1)S(1)}, u32[]{:S(2)}, u32[]{:S(2)}) collective-permute-start(bf16[48,1,128]{2,1,0:T(2,128)(2,1)S(1)} %get-tuple-element.203), channel_id=1, source_target_pairs={{0,1},{1,2},{2,3},{3,4},{4,5},{5,6},{6,7},{7,8},{8,9},{9,10},{10,1... | collective-permute-start | bytes 36872 | tf_op jit(solution)/shard_map/ppermute | solution.py:14
  120.2 5.9 collective-permute-start.4
  126.8 1.2 copy-start.4
  126.8 1.2 copy-start.8
  221.2 0.7 copy-start.1
  222.0 357.5 %all-reduce.5.cloned.1.call-start = ((), (), s32[]{:S(2)}) async-start(), calls=%async_computation.1 | async-start | bytes 172032 | tf_op jit(solution)/shard_map/psum | solution.py:95
Sparse Core Ops, SparseCore 0:
  222.1 38.3 reduce-scatter.3
  263.9 315.4 all-reduce.4
where the time goes:
time: 590 us; the launch traced here: 588 us
  waiting for transfers between devices  426 us (72%)
  local copies, waits for them, and re-layouts  42.7 us (7%)
  starting transfers between devices  41.8 us (7%)
  loops' own time  37.6 us (6%)
  other arithmetic  18.2 us (3%)
  between operations  14.4 us (2%)
  matrix products  7.1 us (1%)
    psum x1, waiting for transfers between devices, body(): total = lax.psum(grad, ('tm', 'tile'))  319 us
    ppermute x7, waiting for transfers between devices, shifted(): return lax.ppermute(block, axis, route)  62.4 us
    unnamed x3, waiting for transfers between devices  38.5 us
    another operation x1, loops' own time, body(): latents, grad = lax.fori_loop(0, count, one_tile, start)  37.4 us
    ppermute x7, starting transfers between devices, shifted(): return lax.ppermute(block, axis, route)  31.3 us
  transfers between devices with their start and end apart: 13, of which 11 were waited for; matrix products, arithmetic and copies ran while one was open for 0% of the time, Pallas kernels for 0%

commit v1 on v0

v1 whole, which is shorter than its diff:
```python
import functools

import jax
import jax.numpy as jnp
from jax import lax
from jax.experimental import pallas as pl
from jax.experimental.pallas import tpu as pltpu
from jax.sharding import PartitionSpec as P

BF = jnp.bfloat16
F32 = jnp.float32
MESH = pl.DeviceIdType.MESH


def z_groups(size):
    return [(1, 4), (4, 4)] if size == 16 else [(1, size)]


def swap_blocks(parts, lane):
    for m in (1, 2, 4):
        low = (lane & (16 * m)) == 0
        done = list(parts)
        for p in range(8):
            if p & m:
                continue
            q = p | m
            done[p] = jnp.where(low, parts[p], pltpu.roll(parts[q], 16 * m, 1))
            done[q] = jnp.where(low, pltpu.roll(parts[p], 128 - 16 * m, 1), parts[q])
        parts = done
    return parts


def store_shifts(out_ref, start, gap, value, lane):
    wide = value.astype(F32)
    before = jnp.where(lane == 0, 0.0, pltpu.roll(wide, 1, 1))
    after = jnp.where(lane == 127, 0.0, pltpu.roll(wide, 127, 1))
    out_ref[pl.ds(start, 48), :] = before.astype(BF)
    out_ref[pl.ds(start + gap, 48), :] = value
    out_ref[pl.ds(start + 2 * gap, 48), :] = after.astype(BF)


def kernel(
    sizes,
    x_hbm, w_in_ref, bias_ref, w_ent_ref, tiles_ref, count_ref, cot_hbm,
    lat_ref, grad_ref,
    xv, xf, xb, cotv, frame_rows, edge_rows, halo, conv_in, state, ctx_out, ctx, ctx_edge,
    joined, cot_dense, lat_dense, lat_tiles, grad_t, pieces, parts, z_out, z_in, final,
    load_sem, main_send, main_recv, edge_send, edge_recv, halo_send, halo_recv,
    ctx_send, ctx_recv, ctx_edge_send, ctx_edge_recv,
    piece_send, piece_recv, z_send, z_recv, final_send, final_recv,
):
    ydim, tdim, zdim = sizes
    y = lax.axis_index("dp")
    t = lax.axis_index("tm")
    b = lax.axis_index("tile")
    above = lax.rem(b + zdim - 1, zdim)
    below = lax.rem(b + 1, zdim)
    plane = ydim * tdim
    spot = y * tdim + t
    per = 32 // tdim
    groups = z_groups(zdim)
    out_rows = 96 // ydim
    pend = []

    def send(cond, make):
        @pl.when(cond)
        def _():
            make().start()

        pend.append((cond, make))

    def remote(src, dst, ssem, rsem, **where):
        return pltpu.make_async_remote_copy(
            src_ref=src, dst_ref=dst, send_sem=ssem, recv_sem=rsem, device_id=where, device_id_type=MESH
        )

    def arrived(ref, sem):
        pltpu.make_async_copy(ref, ref, sem).wait()

    def z_peer(stride, members, d):
        pos = lax.rem(b // stride, members)
        return b + (lax.rem(pos + d, members) - pos) * stride

    load_x = pltpu.make_async_copy(x_hbm, xv, load_sem.at[0])
    load_x.start()
    load_cot = pltpu.make_async_copy(cot_hbm, cotv, load_sem.at[1])
    load_cot.start()

    barrier = pltpu.get_barrier_semaphore()

    @pl.loop(1, plane)
    def _(d):
        peer = lax.rem(spot + d, plane)
        pl.semaphore_signal(
            barrier, inc=1, device_id={"dp": peer // tdim, "tm": lax.rem(peer, tdim)}, device_id_type=MESH
        )

    @pl.loop(0, tdim)
    def _(d):
        pl.semaphore_signal(barrier, inc=1, device_id={"tm": d, "tile": above}, device_id_type=MESH)
        pl.semaphore_signal(barrier, inc=1, device_id={"tm": d, "tile": below}, device_id_type=MESH)

    greeted = plane - 1 + 2 * tdim
    for stride, members in groups:
        for d in range(1, members):
            pl.semaphore_signal(
                barrier, inc=1, device_id={"tile": z_peer(stride, members, d)}, device_id_type=MESH
            )
            greeted += 1

    lane = lax.broadcasted_iota(jnp.int32, (48, 128), 1)
    blank = jnp.zeros((48, 128), BF)

    load_x.wait()
    xf[...] = xv[...].astype(F32).reshape(48 * 32, 128)
    xb[0] = blank
    xb[33] = blank
    for r in range(32):
        xb[1 + r] = xf[pl.ds(r, 48, stride=32), :].astype(BF)

    pl.semaphore_wait(barrier, greeted)

    sends = t < tdim - 1
    for j in range(tdim):
        send(
            sends & (t != j),
            lambda j=j: remote(
                xb.at[pl.ds(per * j, per + 2)], frame_rows.at[t], main_send.at[j], main_recv.at[t], tm=j
            ),
        )
    send(sends, lambda: remote(xb.at[32], edge_rows.at[t], edge_send.at[0], edge_recv.at[t], tm=0, tile=below))
    send(sends, lambda: remote(xb.at[1], edge_rows.at[t], edge_send.at[1], edge_recv.at[t], tm=tdim - 1, tile=above))
    always = t >= 0
    send(always, lambda: remote(xb.at[32], halo.at[0], halo_send.at[0], halo_recv.at[0], tile=below))
    send(always, lambda: remote(xb.at[1], halo.at[1], halo_send.at[1], halo_recv.at[1], tile=above))

    @pl.when(sends)
    def _():
        frame_rows[t] = xb[pl.ds(per * t, per + 2)]

    @pl.loop(1, 33)
    def _(r):
        store_shifts(joined, 288 * r, 96, xb[r], lane)

    load_cot.wait()
    count = count_ref[0]
    slots = []
    for n in range(16):
        found = jnp.int32(0)
        for k in range(12):
            found = jnp.where((tiles_ref[k] == n) & (k < count), k + 1, found)
        slots.append(found)
    for half in range(2):
        for h in range(2):
            columns = slice(128 * h, 128 * h + 128)
            rows = []
            for i in range(8):
                found = slots[8 * half + i]
                held = cotv[jnp.maximum(found - 1, 0), :, columns].astype(F32)
                rows.append(jnp.where(found > 0, held, 0.0))
            for i, row in enumerate(swap_blocks(rows, lane)):
                cot_dense[16 * half + 8 * h + i] = row

    for edge, row, there in ((0, 0, b > 0), (1, 33, b < zdim - 1)):
        arrived(halo.at[edge], halo_recv.at[edge])
        store_shifts(joined, 288 * row, 96, jnp.where(there, halo[edge], blank), lane)

    state[...] = jnp.zeros_like(state)

    @pl.loop(0, tdim - 1)
    def _(f):
        @pl.when(t != f)
        def _():
            arrived(frame_rows.at[f], main_recv.at[f])

        @pl.when(t == 0)
        def _():
            arrived(edge_rows.at[f], edge_recv.at[f])
            frame_rows[f, 0] = jnp.where(b > 0, edge_rows[f], blank)

        @pl.when(t == tdim - 1)
        def _():
            arrived(edge_rows.at[f], edge_recv.at[f])
            frame_rows[f, per + 1] = jnp.where(b < zdim - 1, edge_rows[f], blank)

        for r in range(per + 2):
            store_shifts(conv_in, 144 * r, 48, frame_rows[f, r], lane)
        taps = jnp.concatenate([conv_in[pl.ds(144 * r, 432), :] for r in range(per)], axis=1)
        mixed = jnp.dot(w_in_ref[...], taps, preferred_element_type=F32)
        gate = 0.5 * jnp.tanh(0.5 * (mixed[:48] + bias_ref[...])) + 0.5
        now = gate * state[...] + jnp.tanh(mixed[48:])
        state[...] = now
        for r in range(per):
            ctx_out[f, r] = now[:, 128 * r : 128 * r + 128].astype(BF)

        @pl.when(t != f + 1)
        def _():
            remote(
                ctx_out.at[f], ctx.at[pl.ds(1 + per * t, per)], ctx_send.at[f], ctx_recv.at[t], tm=f + 1
            ).start()

        @pl.when(t == f + 1)
        def _():
            ctx[pl.ds(1 + per * t, per)] = ctx_out[f]

        @pl.when(t == tdim - 1)
        def _():
            remote(
                ctx_out.at[f, per - 1], ctx_edge.at[0], ctx_edge_send.at[f], ctx_edge_recv.at[0],
                tm=f + 1, tile=below,
            ).start()

        @pl.when(t == 0)
        def _():
            remote(
                ctx_out.at[f, 0], ctx_edge.at[1], ctx_edge_send.at[f], ctx_edge_recv.at[1],
                tm=f + 1, tile=above,
            ).start()

    @pl.when(t == 0)
    def _():
        ctx[...] = jnp.zeros_like(ctx)
        ctx_edge[...] = jnp.zeros_like(ctx_edge)

    @pl.when(t > 0)
    def _():
        for j in range(tdim):
            @pl.when(t != j)
            def _():
                arrived(ctx.at[pl.ds(1 + per * j, per)], ctx_recv.at[j])
        for edge in range(2):
            arrived(ctx_edge.at[edge], ctx_edge_recv.at[edge])

    store_shifts(joined, 48, 96, jnp.where(b > 0, ctx_edge[0], blank), lane)
    store_shifts(joined, 288 * 33 + 48, 96, jnp.where(b < zdim - 1, ctx_edge[1], blank), lane)

    @pl.loop(1, 33)
    def _(r):
        store_shifts(joined, 288 * r + 48, 96, ctx[r], lane)

    grad_t[...] = jnp.zeros_like(grad_t)

    @pl.loop(0, 4)
    def _(part):
        base = 8 * part
        taps = jnp.concatenate([joined[pl.ds(288 * (base + r), 864), :] for r in range(8)], axis=1)
        pre = jnp.dot(w_ent_ref[...], taps, preferred_element_type=F32)
        pushes = []
        for r in range(8):
            mean = pre[:48, 128 * r : 128 * r + 128]
            spread = pre[48:, 128 * r : 128 * r + 128]
            small = jnp.exp(-jnp.abs(spread))
            sigma = 0.5 + jnp.maximum(spread, 0.0) + jnp.log(1.0 + small)
            slope = jnp.where(spread >= 0, 1.0, small) / (1.0 + small)
            scale = 1.0 / sigma
            lat = (xb[base + r + 1].astype(F32) - mean) * scale
            lat_dense[base + r] = lat
            near = -cot_dense[base + r] * scale
            pushes.append(jnp.concatenate([near, near * lat * slope], axis=0).astype(BF))
        push = jnp.concatenate(pushes, axis=1)
        grad_t[:864, :96] += lax.dot_general(taps, push, (((1,), (1,)), ((), ())), preferred_element_type=F32)

    for l in range(7):
        block = grad_t[128 * l : 128 * l + 128, :].T
        for other in range(ydim):
            pieces[7 * other + l, :out_rows] = block[out_rows * other : out_rows * (other + 1)].astype(BF)

    @pl.loop(1, plane)
    def _(d):
        peer = lax.rem(spot + d, plane)
        other, l = peer // tdim, lax.rem(peer, tdim)

        @pl.when(l < 7)
        def _():
            remote(pieces.at[7 * other + l], parts.at[spot], piece_send, piece_recv, dp=other, tm=l).start()

    for half in range(2):
        for h in range(2):
            rows = [lat_dense[16 * half + 8 * h + i] for i in range(8)]
            for i, row in enumerate(swap_blocks(rows, lane)):
                lat_tiles[8 * half + i, :, 128 * h : 128 * h + 128] = row.astype(BF)
    for k in range(12):
        held = lat_tiles[tiles_ref[k]]
        lat_ref[k] = jnp.where(k < count, held, jnp.zeros_like(held))

    owner = t < 7

    @pl.when(owner)
    def _():
        parts[spot] = pieces[7 * y + t]
        arrived(parts.at[pl.ds(0, plane - 1)], piece_recv)
        z_out[0] = jnp.zeros_like(z_out.at[0])

        @pl.loop(0, plane)
        def _(i):
            z_out[0] += parts[i].astype(F32)[:out_rows]

        for step, (stride, members) in enumerate(groups):
            for d in range(1, members):
                remote(
                    z_out.at[step], z_in.at[step, d - 1], z_send.at[step, d - 1], z_recv.at[step],
                    tile=z_peer(stride, members, d),
                ).start()
            arrived(z_in.at[step, pl.ds(0, members - 1)], z_recv.at[step])
            total = z_out[step]
            for d in range(1, members):
                total = total + z_in[step, d - 1]
            if step + 1 < len(groups):
                z_out[step + 1] = total
            else:
                final[t] = total
        for d in range(1, tdim):
            remote(
                final.at[t], final.at[t], final_send.at[d - 1], final_recv.at[t], tm=lax.rem(t + d, tdim)
            ).start()

    for l in range(7):
        @pl.when(t != l)
        def _():
            arrived(final.at[l], final_recv.at[l])

        width = min(128, 864 - 128 * l)
        grad_ref[:, 128 * l : 128 * l + width] = final[l][:, :width]

    for cond, make in pend:
        @pl.when(cond)
        def _(make=make):
            make().wait_send()

    @pl.loop(0, tdim - 1)
    def _(f):
        @pl.when(t != f + 1)
        def _():
            arrived(ctx_out.at[f], ctx_send.at[f])

        @pl.when((t == 0) | (t == tdim - 1))
        def _():
            arrived(ctx_out.at[f, 0], ctx_edge_send.at[f])

    @pl.when(owner)
    def _():
        arrived(pieces.at[pl.ds(0, 7 * ydim - 1)], piece_send)
        for step, (stride, members) in enumerate(groups):
            for d in range(1, members):
                arrived(z_out.at[step], z_send.at[step, d - 1])
        for d in range(1, tdim):
            arrived(final.at[t], final_send.at[d - 1])

    @pl.when(t == tdim - 1)
    def _():
        arrived(pieces, piece_send)


def body(sizes, frames_in, w_in, gate_bias, w_ent, active_tiles, active_count, cotangent):
    ydim, tdim, zdim = sizes
    plane = ydim * tdim
    per = 32 // tdim
    groups = z_groups(zdim)
    steps, most = len(groups), max(m for _, m in groups)
    out_rows = 96 // ydim
    held_rows = -(-out_rows // 16) * 16
    vmem = pl.BlockSpec(memory_space=pltpu.VMEM)
    smem = pl.BlockSpec(memory_space=pltpu.SMEM)
    hbm = pl.BlockSpec(memory_space=pl.ANY)
    dma = pltpu.SemaphoreType.DMA
    latent, grad = pl.pallas_call(
        functools.partial(kernel, sizes),
        out_shape=(
            jax.ShapeDtypeStruct((12, 48, 256), BF),
            jax.ShapeDtypeStruct((out_rows, 864), F32),
        ),
        in_specs=[hbm, vmem, vmem, vmem, smem, smem, hbm],
        out_specs=(vmem, vmem),
        scratch_shapes=[
            pltpu.VMEM((48, 32, 128), BF),
            pltpu.VMEM((48 * 32, 128), F32),
            pltpu.VMEM((34, 48, 128), BF),
            pltpu.VMEM((12, 48, 256), BF),
            pltpu.VMEM((tdim, per + 2, 48, 128), BF),
            pltpu.VMEM((tdim, 48, 128), BF),
            pltpu.VMEM((2, 48, 128), BF),
            pltpu.VMEM(((per + 2) * 144, 128), BF),
            pltpu.VMEM((48, per * 128), F32),
            pltpu.VMEM((tdim - 1, per, 48, 128), BF),
            pltpu.VMEM((34, 48, 128), BF),
            pltpu.VMEM((2, 48, 128), BF),
            pltpu.VMEM((34 * 288, 128), BF),
            pltpu.VMEM((32, 48, 128), F32),
            pltpu.VMEM((32, 48, 128), F32),
            pltpu.VMEM((16, 48, 256), BF),
            pltpu.VMEM((896, 128), F32),
            pltpu.VMEM((7 * ydim, held_rows, 128), BF),
            pltpu.VMEM((plane, held_rows, 128), BF),
            pltpu.VMEM((steps, out_rows, 128), F32),
            pltpu.VMEM((steps, most - 1, out_rows, 128), F32),
            pltpu.VMEM((7, out_rows, 128), F32),
            dma((2,)),
            dma((tdim,)), dma((tdim,)),
            dma((2,)), dma((tdim,)),
            dma((2,)), dma((2,)),
            dma((tdim - 1,)), dma((tdim,)),
            dma((tdim - 1,)), dma((2,)),
            dma, dma,
            dma((steps, most - 1)), dma((steps,)),
            dma((tdim - 1,)), dma((7,)),
        ],
        compiler_params=pltpu.CompilerParams(
            collective_id=0, has_side_effects=True, vmem_limit_bytes=32 * 1024 * 1024
        ),
        cost_estimate=pl.CostEstimate(flops=1_700_000_000, bytes_accessed=1_500_000, transcendentals=1_500_000),
        name="coding_window",
    )(
        frames_in[0, 0],
        w_in,
        gate_bias[:, None],
        w_ent,
        active_tiles[0, 0, 0],
        active_count[0, 0],
        cotangent[0, 0, 0],
    )
    return (latent[None, None, None], grad)


def solution(mesh):
    sizes = tuple(mesh.shape[axis] for axis in ("dp", "tm", "tile"))
    return jax.shard_map(
        functools.partial(body, sizes),
        mesh=mesh,
        in_specs=(
            P("dp", "tm", None, "tile", None),
            P(),
            P(),
            P(),
            P("dp", "tm", "tile", None),
            P("dp", "tm", "tile"),
            P("dp", "tm", "tile", None, None, None),
        ),
        out_specs=(P("dp", "tm", "tile", None, None, None), P("dp", None)),
        check_vma=False,
    )
```

time: 590 us -> 66.9 us (0.11)
  waiting for transfers between devices: 426 us -> 0 us
  Pallas kernels: 0 us -> 58.9 us
  starting transfers between devices: 41.8 us -> 0 us
  loops' own time: 37.6 us -> 0 us
  local copies, waits for them, and re-layouts: 42.7 us -> 6.42 us
  other arithmetic: 18.2 us -> 0 us
  between operations: 14.4 us -> 1.3 us
  matrix products: 7.1 us -> 0 us
    psum x1 -> x0, waiting for transfers between devices: 319 us -> none  [body(): total = lax.psum(grad, ('tm', 'tile'))]
    ppermute x11 -> x0, waiting for transfers between devices: 68.6 us -> none  [the longest x7 62.4 us: shifted(): return lax.ppermute(block, axis, route)]
    pallas_call x0 -> x1, Pallas kernels: none -> 58.9 us  [body(): pl.pallas_call(functools.partial(kernel, sizes), out_shape=(jax.ShapeDtyp...]
    ppermute x11 -> x0, starting transfers between devices: 41.8 us -> none  [the longest x7 31.3 us: shifted(): return lax.ppermute(block, axis, route)]
    unnamed x3 -> x0, waiting for transfers between devices: 38.5 us -> none
    another operation x2 -> x0, loops' own time: 37.6 us -> none  [the longest x1 37.4 us: body(): latents, grad = lax.fori_loop(0, count, one_tile, start)]
    dynamic_slice x22 -> x0, local copies, waits for them, and re-layouts: 16.1 us -> none  [the longest x11 9.42 us: one_tile(): lax.dynamic_slice(frame, (0, row0, col0), (chans, 16, 16))]
    another operation x12 -> x0, other arithmetic: 8.94 us -> none
  transfers between devices with their start and end apart: 13 -> 0, of which waited for: 11 -> 0; matrix products, arithmetic and copies ran while one was open for 0% -> 0% of each run, Pallas kernels for 0% -> 0%
where the time goes in v1:
time: 66.9 us; the launch traced here: 66.6 us
  Pallas kernels  58.9 us (88%)
  local copies, waits for them, and re-layouts  6.42 us (10%)
  between operations  1.3 us (2%)
    pallas_call x1, Pallas kernels, body(): pl.pallas_call(functools.partial(kernel, sizes), out_shape=(jax.ShapeDtyp...  58.9 us
    unnamed x14, local copies, waits for them, and re-layouts  6.33 us

profile of v1, /device:TPU:1, one launch (start us, length us, event | category | flops | bytes accessed | tf_op | source)
XLA Modules:
  0.0 66.6 jit_solution(13563276664853825666)
XLA Ops:
  1.3 0.0 copy-start.5
  1.3 0.6 copy-done.5
  1.9 0.0 copy-start.4
  1.9 0.1 copy.9.bias_ref
  2.0 0.6 copy-done.4
  2.6 0.0 copy-start
  2.6 1.0 %copy-done = bf16[1,1,48,32,128]{4,3,2,1,0:T(8,128)(2,1)S(1)} copy-done((bf16[1,1,48,32,128]{4,3,2,1,0:T(8,128)(2,1)S(1)}, bf16[1,1,48,32,128]{4,3,2,1,0:T(8,128)(2,1)}, u32[]{:S(2)}) %copy-start) | copy-done | bytes 393240
  3.6 0.0 copy-start.1
  3.6 1.0 %copy-done.1 = bf16[1,1,1,12,48,256]{5,4,3,2,1,0:T(8,128)(2,1)S(1)} copy-done((bf16[1,1,1,12,48,256]{5,4,3,2,1,0:T(8,128)(2,1)S(1)}, bf16[1,1,1,12,48,256]{5,4,3,2,1,0:T(8,128)(2,1)}, u32[]{:S(2)}) %copy-start.1) | copy-done | bytes 294936
  4.5 0.0 copy-start.2
  4.5 0.9 %copy-done.2 = bf16[96,864]{1,0:T(8,128)(2,1)S(1)} copy-done((bf16[96,864]{1,0:T(8,128)(2,1)S(1)}, bf16[96,864]{1,0:T(8,128)(2,1)}, u32[]{:S(2)}) %copy-start.2) | copy-done | bytes 165912
  5.5 0.0 copy-start.3
  5.5 0.9 %copy-done.3 = bf16[96,432]{1,0:T(8,128)(2,1)S(1)} copy-done((bf16[96,432]{1,0:T(8,128)(2,1)S(1)}, bf16[96,432]{1,0:T(8,128)(2,1)}, u32[]{:S(2)}) %copy-start.3) | copy-done | bytes 82968
  6.4 58.9 %coding_window.1 = (bf16[12,48,256]{2,1,0:T(8,128)(2,1)S(1)}, f32[24,864]{1,0:T(8,128)S(1)}) custom-call(bf16[48,32,128]{2,1,0:T(8,128)(2,1)S(1)} %bitcast.8, bf16[96,432]{1,0:T(8,128)(2,1)S(1)} %copy-done.3, f32[48,1]{1,0:T(8,128)S(1)} %copy.9.bias_ref, bf16[96,864]{1,0:T(8,128)(2,1)S(1)} %copy-done.2, s32[12]{0:T(128)S(1)} %bitcast.10, ...), custom_call_target="tpu_custom_call" | custom-call | flops 1700000000 | bytes 1500000 | tf_op jit(solution)/shard_map/coding_window/pallas_call | solution.py:366
  65.3 0.7 %copy.13 = bf16[1,1,1,12,48,256]{5,4,3,2,1,0:T(8,128)(2,1)} copy(bf16[1,1,1,12,48,256]{5,4,3,2,1,0:T(8,128)(2,1)S(1)} %bitcast.7) | data formatting | bytes 589824
  66.0 0.6 copy.14
Async XLA Ops:
  1.3 0.7 copy-start.5
  1.9 0.7 copy-start.4
  2.6 1.0 %copy-start = (bf16[1,1,48,32,128]{4,3,2,1,0:T(8,128)(2,1)S(1)}, bf16[1,1,48,32,128]{4,3,2,1,0:T(8,128)(2,1)}, u32[]{:S(2)}) copy-start(bf16[1,1,48,32,128]{4,3,2,1,0:T(8,128)(2,1)} %param.7) | copy-start | bytes 1179652
  3.6 1.0 %copy-start.1 = (bf16[1,1,1,12,48,256]{5,4,3,2,1,0:T(8,128)(2,1)S(1)}, bf16[1,1,1,12,48,256]{5,4,3,2,1,0:T(8,128)(2,1)}, u32[]{:S(2)}) copy-start(bf16[1,1,1,12,48,256]{5,4,3,2,1,0:T(8,128)(2,1)} %param.13) | copy-start | bytes 884740
  4.5 0.9 %copy-start.2 = (bf16[96,864]{1,0:T(8,128)(2,1)S(1)}, bf16[96,864]{1,0:T(8,128)(2,1)}, u32[]{:S(2)}) copy-start(bf16[96,864]{1,0:T(8,128)(2,1)} %w_ent_ref.1) | copy-start | bytes 497668
  5.5 0.9 %copy-start.3 = (bf16[96,432]{1,0:T(8,128)(2,1)S(1)}, bf16[96,432]{1,0:T(8,128)(2,1)}, u32[]{:S(2)}) copy-start(bf16[96,432]{1,0:T(8,128)(2,1)} %w_in_ref.1) | copy-start | bytes 248836

commit v2 on v1

--- a/solution.py
+++ b/solution.py
@@ -12,8 +12,10 @@
 MESH = pl.DeviceIdType.MESH
 
 
-def z_groups(size):
-    return [(1, 4), (4, 4)] if size == 16 else [(1, size)]
+def z_steps(size):
+    if size == 16:
+        return [((1, 15, 14), True), ((2, 14, 6, 10), False)]
+    return [(tuple(range(1, size)), True)]
 
 
 def swap_blocks(parts, lane):
@@ -41,10 +43,11 @@
 
 def kernel(
     sizes,
-    x_hbm, w_in_ref, bias_ref, w_ent_ref, tiles_ref, count_ref, cot_hbm,
+    x_hbm, w_in_hbm, bias_hbm, w_ent_hbm, tiles_hbm, count_hbm, cot_hbm,
     lat_ref, grad_ref,
+    w_in_ref, bias_ref, w_ent_ref, tiles_ref, count_ref,
     xv, xf, xb, cotv, frame_rows, edge_rows, halo, conv_in, state, ctx_out, ctx, ctx_edge,
-    joined, cot_dense, lat_dense, lat_tiles, grad_t, pieces, parts, z_out, z_in, final,
+    w_part, pre_x, joined, cot_dense, push, lat_dense, lat_tiles, grad_all, pieces, parts, z_out, z_in, final,
     load_sem, main_send, main_recv, edge_send, edge_recv, halo_send, halo_recv,
     ctx_send, ctx_recv, ctx_edge_send, ctx_edge_recv,
     piece_send, piece_recv, z_send, z_recv, final_send, final_recv,
@@ -58,7 +61,7 @@
     plane = ydim * tdim
     spot = y * tdim + t
     per = 32 // tdim
-    groups = z_groups(zdim)
+    steps = z_steps(zdim)
     out_rows = 96 // ydim
     pend = []
 
@@ -77,14 +80,17 @@
     def arrived(ref, sem):
         pltpu.make_async_copy(ref, ref, sem).wait()
 
-    def z_peer(stride, members, d):
-        pos = lax.rem(b // stride, members)
-        return b + (lax.rem(pos + d, members) - pos) * stride
-
-    load_x = pltpu.make_async_copy(x_hbm, xv, load_sem.at[0])
-    load_x.start()
-    load_cot = pltpu.make_async_copy(cot_hbm, cotv, load_sem.at[1])
-    load_cot.start()
+    loads = [
+        pltpu.make_async_copy(src, dst, load_sem.at[i])
+        for i, (src, dst) in enumerate(
+            (
+                (x_hbm, xv), (tiles_hbm, tiles_ref), (count_hbm, count_ref), (cot_hbm, cotv),
+                (w_in_hbm, w_in_ref), (bias_hbm, bias_ref), (w_ent_hbm, w_ent_ref),
+            )
+        )
+    ]
+    for load in loads:
+        load.start()
 
     barrier = pltpu.get_barrier_semaphore()
 
@@ -101,17 +107,14 @@
         pl.semaphore_signal(barrier, inc=1, device_id={"tm": d, "tile": below}, device_id_type=MESH)
 
     greeted = plane - 1 + 2 * tdim
-    for stride, members in groups:
-        for d in range(1, members):
-            pl.semaphore_signal(
-                barrier, inc=1, device_id={"tile": z_peer(stride, members, d)}, device_id_type=MESH
-            )
-            greeted += 1
+    for d in sorted({d for offsets, _ in steps for d in offsets} - {1, zdim - 1}):
+        pl.semaphore_signal(barrier, inc=1, device_id={"tile": lax.rem(b + d, zdim)}, device_id_type=MESH)
+        greeted += 1
 
     lane = lax.broadcasted_iota(jnp.int32, (48, 128), 1)
     blank = jnp.zeros((48, 128), BF)
 
-    load_x.wait()
+    loads[0].wait()
     xf[...] = xv[...].astype(F32).reshape(48 * 32, 128)
     xb[0] = blank
     xb[33] = blank
@@ -121,15 +124,16 @@
     pl.semaphore_wait(barrier, greeted)
 
     sends = t < tdim - 1
-    for j in range(tdim):
+    send(sends, lambda: remote(xb.at[32], edge_rows.at[t], edge_send.at[0], edge_recv.at[t], tm=0, tile=below))
+    send(sends, lambda: remote(xb.at[1], edge_rows.at[t], edge_send.at[1], edge_recv.at[t], tm=tdim - 1, tile=above))
+    for d in range(1, tdim):
+        j = lax.rem(t + d, tdim)
         send(
-            sends & (t != j),
-            lambda j=j: remote(
-                xb.at[pl.ds(per * j, per + 2)], frame_rows.at[t], main_send.at[j], main_recv.at[t], tm=j
+            sends,
+            lambda d=d, j=j: remote(
+                xb.at[pl.ds(per * j, per + 2)], frame_rows.at[t], main_send.at[d], main_recv.at[t], tm=j
             ),
         )
-    send(sends, lambda: remote(xb.at[32], edge_rows.at[t], edge_send.at[0], edge_recv.at[t], tm=0, tile=below))
-    send(sends, lambda: remote(xb.at[1], edge_rows.at[t], edge_send.at[1], edge_recv.at[t], tm=tdim - 1, tile=above))
     always = t >= 0
     send(always, lambda: remote(xb.at[32], halo.at[0], halo_send.at[0], halo_recv.at[0], tile=below))
     send(always, lambda: remote(xb.at[1], halo.at[1], halo_send.at[1], halo_recv.at[1], tile=above))
@@ -138,17 +142,17 @@
     def _():
         frame_rows[t] = xb[pl.ds(per * t, per + 2)]
 
-    @pl.loop(1, 33)
-    def _(r):
+    for r in range(1, 33):
         store_shifts(joined, 288 * r, 96, xb[r], lane)
 
-    load_cot.wait()
-    count = count_ref[0]
+    for load in loads[1:4]:
+        load.wait()
+    count = count_ref[0, 0, 0]
     slots = []
     for n in range(16):
         found = jnp.int32(0)
         for k in range(12):
-            found = jnp.where((tiles_ref[k] == n) & (k < count), k + 1, found)
+            found = jnp.where((tiles_ref[0, k] == n) & (k < count), k + 1, found)
         slots.append(found)
     for half in range(2):
         for h in range(2):
@@ -165,7 +169,23 @@
         arrived(halo.at[edge], halo_recv.at[edge])
         store_shifts(joined, 288 * row, 96, jnp.where(there, halo[edge], blank), lane)
 
+    loads[6].wait()
+    w_all = w_ent_ref[...]
+    for part in range(2):
+        w_part[part] = jnp.concatenate([w_all[:, 96 * k + 48 * part : 96 * k + 48 * part + 48] for k in range(9)], axis=1)
+
+    def taps(part, r):
+        starts = [288 * (r + dy) + 96 * dx + 48 * part for dy in range(3) for dx in range(3)]
+        return jnp.concatenate([joined[start : start + 48, :] for start in starts], axis=0)
+
+    for block in range(2):
+        cells = jnp.concatenate([taps(0, 16 * block + r) for r in range(16)], axis=1)
+        pre_x[block] = jnp.dot(w_part[0], cells, preferred_element_type=F32)
+
     state[...] = jnp.zeros_like(state)
+    for load in loads[4:6]:
+        load.wait()
+    bias = bias_ref[...].T[:48, :1]
 
     @pl.loop(0, tdim - 1)
     def _(f):
@@ -185,9 +205,9 @@
 
         for r in range(per + 2):
             store_shifts(conv_in, 144 * r, 48, frame_rows[f, r], lane)
-        taps = jnp.concatenate([conv_in[pl.ds(144 * r, 432), :] for r in range(per)], axis=1)
-        mixed = jnp.dot(w_in_ref[...], taps, preferred_element_type=F32)
-        gate = 0.5 * jnp.tanh(0.5 * (mixed[:48] + bias_ref[...])) + 0.5
+        cells = jnp.concatenate([conv_in[pl.ds(144 * r, 432), :] for r in range(per)], axis=1)
+        mixed = jnp.dot(w_in_ref[...], cells, preferred_element_type=F32)
+        gate = 0.5 * jnp.tanh(0.5 * (mixed[:48] + bias)) + 0.5
         now = gate * state[...] + jnp.tanh(mixed[48:])
         state[...] = now
         for r in range(per):
@@ -222,48 +242,58 @@
         ctx[...] = jnp.zeros_like(ctx)
         ctx_edge[...] = jnp.zeros_like(ctx_edge)
 
-    @pl.when(t > 0)
-    def _():
-        for j in range(tdim):
-            @pl.when(t != j)
-            def _():
-                arrived(ctx.at[pl.ds(1 + per * j, per)], ctx_recv.at[j])
-        for edge in range(2):
+    for j in range(tdim):
+        @pl.when((t > 0) & (t != j))
+        def _():
+            arrived(ctx.at[pl.ds(1 + per * j, per)], ctx_recv.at[j])
+
+        for r in range(1 + per * j, 1 + per * (j + 1)):
+            store_shifts(joined, 288 * r + 48, 96, ctx[r], lane)
+
+    for edge, row, there in ((0, 0, b > 0), (1, 33, b < zdim - 1)):
+        @pl.when(t > 0)
+        def _():
             arrived(ctx_edge.at[edge], ctx_edge_recv.at[edge])
 
-    store_shifts(joined, 48, 96, jnp.where(b > 0, ctx_edge[0], blank), lane)
-    store_shifts(joined, 288 * 33 + 48, 96, jnp.where(b < zdim - 1, ctx_edge[1], blank), lane)
-
-    @pl.loop(1, 33)
-    def _(r):
-        store_shifts(joined, 288 * r + 48, 96, ctx[r], lane)
-
-    grad_t[...] = jnp.zeros_like(grad_t)
-
-    @pl.loop(0, 4)
-    def _(part):
-        base = 8 * part
-        taps = jnp.concatenate([joined[pl.ds(288 * (base + r), 864), :] for r in range(8)], axis=1)
-        pre = jnp.dot(w_ent_ref[...], taps, preferred_element_type=F32)
-        pushes = []
-        for r in range(8):
-            mean = pre[:48, 128 * r : 128 * r + 128]
-            spread = pre[48:, 128 * r : 128 * r + 128]
+        store_shifts(joined, 288 * row + 48, 96, jnp.where(there, ctx_edge[edge], blank), lane)
+
+    for r in (-2, -1, 32, 33):
+        push[96 * (33 - r) : 96 * (34 - r), :] = jnp.zeros((96, 128), BF)
+    for block in range(2):
+        cells = jnp.concatenate([taps(1, 16 * block + r) for r in range(16)], axis=1)
+        pre = pre_x[block] + jnp.dot(w_part[1], cells, preferred_element_type=F32)
+        for i in range(16):
+            r = 16 * block + i
+            mean = pre[:48, 128 * i : 128 * i + 128]
+            spread = pre[48:, 128 * i : 128 * i + 128]
             small = jnp.exp(-jnp.abs(spread))
             sigma = 0.5 + jnp.maximum(spread, 0.0) + jnp.log(1.0 + small)
             slope = jnp.where(spread >= 0, 1.0, small) / (1.0 + small)
             scale = 1.0 / sigma
-            lat = (xb[base + r + 1].astype(F32) - mean) * scale
-            lat_dense[base + r] = lat
-            near = -cot_dense[base + r] * scale
-            pushes.append(jnp.concatenate([near, near * lat * slope], axis=0).astype(BF))
-        push = jnp.concatenate(pushes, axis=1)
-        grad_t[:864, :96] += lax.dot_general(taps, push, (((1,), (1,)), ((), ())), preferred_element_type=F32)
-
-    for l in range(7):
-        block = grad_t[128 * l : 128 * l + 128, :].T
-        for other in range(ydim):
-            pieces[7 * other + l, :out_rows] = block[out_rows * other : out_rows * (other + 1)].astype(BF)
+            lat = (xb[r + 1].astype(F32) - mean) * scale
+            lat_dense[r] = lat
+            near = -cot_dense[r] * scale
+            push[96 * (33 - r) : 96 * (33 - r) + 48, :] = near.astype(BF)
+            push[96 * (33 - r) + 48 : 96 * (34 - r), :] = (near * lat * slope).astype(BF)
+
+    for first, last in ((0, 18), (18, 34)):
+        near = jnp.concatenate([push[96 * (33 - r) : 96 * (36 - r), :] for r in range(first, last)], axis=1)
+        rows = jnp.concatenate([joined[288 * r : 288 * r + 288, :] for r in range(first, last)], axis=1)
+        term = lax.dot_general(near, rows, (((1,), (1,)), ((), ())), preferred_element_type=F32)
+        if first == 0:
+            grad_all[...] = term
+        else:
+            grad_all[...] += term
+
+    for other in range(ydim):
+        tails = []
+        for dy in range(3):
+            block = grad_all[96 * dy + out_rows * other : 96 * dy + out_rows * (other + 1), :]
+            pieces[7 * other + 2 * dy, :out_rows] = block[:, :128].astype(BF)
+            pieces[7 * other + 2 * dy + 1, :out_rows] = block[:, 128:256].astype(BF)
+            tails.append(block[:, 256:])
+        tails.append(jnp.zeros_like(tails[0]))
+        pieces[7 * other + 6, :out_rows] = jnp.concatenate(tails, axis=1).astype(BF)
 
     @pl.loop(1, plane)
     def _(d):
@@ -280,7 +310,7 @@
             for i, row in enumerate(swap_blocks(rows, lane)):
                 lat_tiles[8 * half + i, :, 128 * h : 128 * h + 128] = row.astype(BF)
     for k in range(12):
-        held = lat_tiles[tiles_ref[k]]
+        held = lat_tiles[tiles_ref[0, k]]
         lat_ref[k] = jnp.where(k < count, held, jnp.zeros_like(held))
 
     owner = t < 7
@@ -289,23 +319,22 @@
     def _():
         parts[spot] = pieces[7 * y + t]
         arrived(parts.at[pl.ds(0, plane - 1)], piece_recv)
-        z_out[0] = jnp.zeros_like(z_out.at[0])
-
-        @pl.loop(0, plane)
-        def _(i):
-            z_out[0] += parts[i].astype(F32)[:out_rows]
-
-        for step, (stride, members) in enumerate(groups):
-            for d in range(1, members):
+        total = jnp.zeros_like(z_out.at[0])
+        for i in range(plane):
+            total = total + parts[i].astype(F32)[:out_rows]
+        z_out[0] = total
+
+        for step, (offsets, own) in enumerate(steps):
+            for i, d in enumerate(offsets):
                 remote(
-                    z_out.at[step], z_in.at[step, d - 1], z_send.at[step, d - 1], z_recv.at[step],
-                    tile=z_peer(stride, members, d),
+                    z_out.at[step], z_in.at[step, i], z_send.at[step, i], z_recv.at[step],
+                    tile=lax.rem(b + d, zdim),
                 ).start()
-            arrived(z_in.at[step, pl.ds(0, members - 1)], z_recv.at[step])
-            total = z_out[step]
-            for d in range(1, members):
-                total = total + z_in[step, d - 1]
-            if step + 1 < len(groups):
+            arrived(z_in.at[step, pl.ds(0, len(offsets))], z_recv.at[step])
+            total = z_out[step] if own else jnp.zeros_like(z_out.at[step])
+            for i in range(len(offsets)):
+                total = total + z_in[step, i]
+            if step + 1 < len(steps):
                 z_out[step + 1] = total
             else:
                 final[t] = total
@@ -319,8 +348,10 @@
         def _():
             arrived(final.at[l], final_recv.at[l])
 
-        width = min(128, 864 - 128 * l)
-        grad_ref[:, 128 * l : 128 * l + width] = final[l][:, :width]
+    for dy in range(3):
+        grad_ref[:, 288 * dy : 288 * (dy + 1)] = jnp.concatenate(
+            [final[2 * dy], final[2 * dy + 1], final[6][:, 32 * dy : 32 * (dy + 1)]], axis=1
+        )
 
     for cond, make in pend:
         @pl.when(cond)
@@ -340,9 +371,9 @@
     @pl.when(owner)
     def _():
         arrived(pieces.at[pl.ds(0, 7 * ydim - 1)], piece_send)
-        for step, (stride, members) in enumerate(groups):
-            for d in range(1, members):
-                arrived(z_out.at[step], z_send.at[step, d - 1])
+        for step, (offsets, _) in enumerate(steps):
+            for i in range(len(offsets)):
+                arrived(z_out.at[step], z_send.at[step, i])
         for d in range(1, tdim):
             arrived(final.at[t], final_send.at[d - 1])
 
@@ -355,13 +386,12 @@
     ydim, tdim, zdim = sizes
     plane = ydim * tdim
     per = 32 // tdim
-    groups = z_groups(zdim)
-    steps, most = len(groups), max(m for _, m in groups)
+    steps = len(z_steps(zdim))
+    most = max(len(offsets) for offsets, _ in z_steps(zdim))
     out_rows = 96 // ydim
     held_rows = -(-out_rows // 16) * 16
     vmem = pl.BlockSpec(memory_space=pltpu.VMEM)
-    smem = pl.BlockSpec(memory_space=pltpu.SMEM)
-    hbm = pl.BlockSpec(memory_space=pl.ANY)
+    hbm = pl.BlockSpec(memory_space=pltpu.HBM)
     dma = pltpu.SemaphoreType.DMA
     latent, grad = pl.pallas_call(
         functools.partial(kernel, sizes),
@@ -369,9 +399,14 @@
             jax.ShapeDtypeStruct((12, 48, 256), BF),
             jax.ShapeDtypeStruct((out_rows, 864), F32),
         ),
-        in_specs=[hbm, vmem, vmem, vmem, smem, smem, hbm],
+        in_specs=[hbm] * 7,
         out_specs=(vmem, vmem),
         scratch_shapes=[
+            pltpu.VMEM((96, 432), BF),
+            pltpu.VMEM((1, 48), F32),
+            pltpu.VMEM((96, 864), BF),
+            pltpu.SMEM((1, 12), jnp.int32),
+            pltpu.SMEM((1, 1, 1), jnp.int32),
             pltpu.VMEM((48, 32, 128), BF),
             pltpu.VMEM((48 * 32, 128), F32),
             pltpu.VMEM((34, 48, 128), BF),
@@ -384,24 +419,27 @@
             pltpu.VMEM((tdim - 1, per, 48, 128), BF),
             pltpu.VMEM((34, 48, 128), BF),
             pltpu.VMEM((2, 48, 128), BF),
+            pltpu.VMEM((2, 96, 432), BF),
+            pltpu.VMEM((2, 96, 2048), F32),
             pltpu.VMEM((34 * 288, 128), BF),
             pltpu.VMEM((32, 48, 128), F32),
+            pltpu.VMEM((36 * 96, 128), BF),
             pltpu.VMEM((32, 48, 128), F32),
             pltpu.VMEM((16, 48, 256), BF),
-            pltpu.VMEM((896, 128), F32),
+            pltpu.VMEM((288, 288), F32),
             pltpu.VMEM((7 * ydim, held_rows, 128), BF),
             pltpu.VMEM((plane, held_rows, 128), BF),
             pltpu.VMEM((steps, out_rows, 128), F32),
-            pltpu.VMEM((steps, most - 1, out_rows, 128), F32),
+            pltpu.VMEM((steps, most, out_rows, 128), F32),
             pltpu.VMEM((7, out_rows, 128), F32),
-            dma((2,)),
+            dma((7,)),
             dma((tdim,)), dma((tdim,)),
             dma((2,)), dma((tdim,)),
             dma((2,)), dma((2,)),
             dma((tdim - 1,)), dma((tdim,)),
             dma((tdim - 1,)), dma((2,)),
             dma, dma,
-            dma((steps, most - 1)), dma((steps,)),
+            dma((steps, most)), dma((steps,)),
             dma((tdim - 1,)), dma((7,)),
         ],
         compiler_params=pltpu.CompilerParams(
@@ -410,13 +448,13 @@
         cost_estimate=pl.CostEstimate(flops=1_700_000_000, bytes_accessed=1_500_000, transcendentals=1_500_000),
         name="coding_window",
     )(
-        frames_in[0, 0],
-        w_in,
-        gate_bias[:, None],
-        w_ent,
-        active_tiles[0, 0, 0],
-        active_count[0, 0],
-        cotangent[0, 0, 0],
+        pltpu.with_memory_space_constraint(frames_in[0, 0], pltpu.HBM),
+        pltpu.with_memory_space_constraint(w_in, pltpu.HBM),
+        pltpu.with_memory_space_constraint(gate_bias[None], pltpu.HBM),
+        pltpu.with_memory_space_constraint(w_ent, pltpu.HBM),
+        pltpu.with_memory_space_constraint(active_tiles[0, 0], pltpu.HBM),
+        active_count,
+        pltpu.with_memory_space_constraint(cotangent[0, 0, 0], pltpu.HBM),
     )
     return (latent[None, None, None], grad)
 

time: 66.9 us -> 57.6 us (0.86)
  local copies, waits for them, and re-layouts: 6.42 us -> 1.35 us
  Pallas kernels: 58.9 us -> 54.8 us
    unnamed x14 -> x2, local copies, waits for them, and re-layouts: 6.33 us -> 1.35 us
    pallas_call x1, Pallas kernels: 58.9 us -> 54.8 us  [body(): pl.pallas_call(functools.partial(kernel, sizes), out_shape=(jax.ShapeDtyp...]
where the time goes in v2:
time: 57.6 us; the launch traced here: 57.4 us
  Pallas kernels  54.8 us (95%)
  local copies, waits for them, and re-layouts  1.35 us (2%)
  between operations  1.29 us (2%)
    pallas_call x1, Pallas kernels, body(): pl.pallas_call(functools.partial(kernel, sizes), out_shape=(jax.ShapeDtyp...  54.8 us
    unnamed x2, local copies, waits for them, and re-layouts  1.35 us

profile of v2, /device:TPU:1, one launch (start us, length us, event | category | flops | bytes accessed | tf_op | source)
XLA Modules:
  0.0 57.4 jit_solution(648850976975952652)
XLA Ops:
  1.3 54.8 %coding_window.1 = (bf16[12,48,256]{2,1,0:T(8,128)(2,1)S(1)}, f32[24,864]{1,0:T(8,128)S(1)}) custom-call(bf16[48,32,128]{2,1,0:T(8,128)(2,1)} %bitcast.6, bf16[96,432]{1,0:T(8,128)(2,1)} %w_in_hbm.1, f32[1,48]{1,0:T(1,128)} %bitcast.8, bf16[96,864]{1,0:T(8,128)(2,1)} %w_ent_hbm.1, s32[1,12]{1,0:T(1,128)} %bitcast.9, s32[1,1,1]{2,1,0:T(1,128)S(6)} %copy.11.count_hbm, ...), custom_call_target="tpu_custom_call" | custom-call | flops 1700000000 | bytes 1500000 | tf_op jit(solution)/shard_map/coding_window/pallas_call | solution.py:396
  56.1 0.7 %copy.12 = bf16[1,1,1,12,48,256]{5,4,3,2,1,0:T(8,128)(2,1)} copy(bf16[1,1,1,12,48,256]{5,4,3,2,1,0:T(8,128)(2,1)S(1)} %bitcast.5) | data formatting | bytes 589824
  56.8 0.6 %copy.13 = f32[24,864]{1,0:T(8,128)} copy(f32[24,864]{1,0:T(8,128)S(1)} %get-tuple-element.9) | data formatting | bytes 165888

commit v3 on v2

--- a/solution.py
+++ b/solution.py
@@ -12,10 +12,11 @@
 MESH = pl.DeviceIdType.MESH
 
 
-def z_steps(size):
-    if size == 16:
-        return [((1, 15, 14), True), ((2, 14, 6, 10), False)]
-    return [(tuple(range(1, size)), True)]
+REACH = 3
+
+
+def relays(size):
+    return max(0, -(-(size // 2) // REACH) - 1)
 
 
 def swap_blocks(parts, lane):
@@ -47,10 +48,10 @@
     lat_ref, grad_ref,
     w_in_ref, bias_ref, w_ent_ref, tiles_ref, count_ref,
     xv, xf, xb, cotv, frame_rows, edge_rows, halo, conv_in, state, ctx_out, ctx, ctx_edge,
-    w_part, pre_x, joined, cot_dense, push, lat_dense, lat_tiles, grad_all, pieces, parts, z_out, z_in, final,
+    w_part, pre_x, joined, cot_dense, push, lat_dense, lat_tiles, grad_all, pieces, parts, z_in, final,
     load_sem, main_send, main_recv, edge_send, edge_recv, halo_send, halo_recv,
     ctx_send, ctx_recv, ctx_edge_send, ctx_edge_recv,
-    piece_send, piece_recv, z_send, z_recv, final_send, final_recv,
+    piece_send, piece_recv, z_send, z_recv, final_send, final_recv, relay_sem,
 ):
     ydim, tdim, zdim = sizes
     y = lax.axis_index("dp")
@@ -61,7 +62,7 @@
     plane = ydim * tdim
     spot = y * tdim + t
     per = 32 // tdim
-    steps = z_steps(zdim)
+    rounds = relays(zdim)
     out_rows = 96 // ydim
     pend = []
 
@@ -107,7 +108,9 @@
         pl.semaphore_signal(barrier, inc=1, device_id={"tm": d, "tile": below}, device_id_type=MESH)
 
     greeted = plane - 1 + 2 * tdim
-    for d in sorted({d for offsets, _ in steps for d in offsets} - {1, zdim - 1}):
+    for d in range(2, zdim - 1):
+        if min(d, zdim - d) > REACH:
+            continue
         pl.semaphore_signal(barrier, inc=1, device_id={"tile": lax.rem(b + d, zdim)}, device_id_type=MESH)
         greeted += 1
 
@@ -122,6 +125,15 @@
         xb[1 + r] = xf[pl.ds(r, 48, stride=32), :].astype(BF)
 
     pl.semaphore_wait(barrier, greeted)
+
+    def relay(step):
+        for d in (REACH, zdim - REACH):
+            pl.semaphore_signal(
+                relay_sem.at[step], inc=1, device_id={"tile": lax.rem(b + d, zdim)}, device_id_type=MESH
+            )
+
+    if rounds > 0:
+        relay(0)
 
     sends = t < tdim - 1
     send(sends, lambda: remote(xb.at[32], edge_rows.at[t], edge_send.at[0], edge_recv.at[t], tm=0, tile=below))
@@ -182,6 +194,10 @@
         cells = jnp.concatenate([taps(0, 16 * block + r) for r in range(16)], axis=1)
         pre_x[block] = jnp.dot(w_part[0], cells, preferred_element_type=F32)
 
+    for step in range(1, rounds):
+        pl.semaphore_wait(relay_sem.at[step - 1], 2)
+        relay(step)
+
     state[...] = jnp.zeros_like(state)
     for load in loads[4:6]:
         load.wait()
@@ -236,6 +252,9 @@
                 ctx_out.at[f, 0], ctx_edge.at[1], ctx_edge_send.at[f], ctx_edge_recv.at[1],
                 tm=f + 1, tile=above,
             ).start()
+
+    if rounds > 0:
+        pl.semaphore_wait(relay_sem.at[rounds - 1], 2)
 
     @pl.when(t == 0)
     def _():
@@ -319,25 +338,17 @@
     def _():
         parts[spot] = pieces[7 * y + t]
         arrived(parts.at[pl.ds(0, plane - 1)], piece_recv)
-        total = jnp.zeros_like(z_out.at[0])
-        for i in range(plane):
-            total = total + parts[i].astype(F32)[:out_rows]
-        z_out[0] = total
-
-        for step, (offsets, own) in enumerate(steps):
-            for i, d in enumerate(offsets):
-                remote(
-                    z_out.at[step], z_in.at[step, i], z_send.at[step, i], z_recv.at[step],
-                    tile=lax.rem(b + d, zdim),
-                ).start()
-            arrived(z_in.at[step, pl.ds(0, len(offsets))], z_recv.at[step])
-            total = z_out[step] if own else jnp.zeros_like(z_out.at[step])
-            for i in range(len(offsets)):
-                total = total + z_in[step, i]
-            if step + 1 < len(steps):
-                z_out[step + 1] = total
-            else:
-                final[t] = total
+        total = parts[0].astype(F32)
+        for i in range(1, plane):
+            total = total + parts[i].astype(F32)
+        z_in[b] = total.astype(BF)
+        for d in sorted(range(1, zdim), key=lambda d: -min(d, zdim - d)):
+            remote(z_in.at[b], z_in.at[b], z_send.at[d], z_recv, tile=lax.rem(b + d, zdim)).start()
+        arrived(z_in.at[pl.ds(0, zdim - 1)], z_recv)
+        total = z_in[0].astype(F32)
+        for i in range(1, zdim):
+            total = total + z_in[i].astype(F32)
+        final[t] = total[:out_rows]
         for d in range(1, tdim):
             remote(
                 final.at[t], final.at[t], final_send.at[d - 1], final_recv.at[t], tm=lax.rem(t + d, tdim)
@@ -371,9 +382,8 @@
     @pl.when(owner)
     def _():
         arrived(pieces.at[pl.ds(0, 7 * ydim - 1)], piece_send)
-        for step, (offsets, _) in enumerate(steps):
-            for i in range(len(offsets)):
-                arrived(z_out.at[step], z_send.at[step, i])
+        for d in range(1, zdim):
+            arrived(z_in.at[b], z_send.at[d])
         for d in range(1, tdim):
             arrived(final.at[t], final_send.at[d - 1])
 
@@ -386,8 +396,6 @@
     ydim, tdim, zdim = sizes
     plane = ydim * tdim
     per = 32 // tdim
-    steps = len(z_steps(zdim))
-    most = max(len(offsets) for offsets, _ in z_steps(zdim))
     out_rows = 96 // ydim
     held_rows = -(-out_rows // 16) * 16
     vmem = pl.BlockSpec(memory_space=pltpu.VMEM)
@@ -429,8 +437,7 @@
             pltpu.VMEM((288, 288), F32),
             pltpu.VMEM((7 * ydim, held_rows, 128), BF),
             pltpu.VMEM((plane, held_rows, 128), BF),
-            pltpu.VMEM((steps, out_rows, 128), F32),
-            pltpu.VMEM((steps, most, out_rows, 128), F32),
+            pltpu.VMEM((zdim, held_rows, 128), BF),
             pltpu.VMEM((7, out_rows, 128), F32),
             dma((7,)),
             dma((tdim,)), dma((tdim,)),
@@ -439,8 +446,9 @@
             dma((tdim - 1,)), dma((tdim,)),
             dma((tdim - 1,)), dma((2,)),
             dma, dma,
-            dma((steps, most)), dma((steps,)),
+            dma((zdim,)), dma,
             dma((tdim - 1,)), dma((7,)),
+            pltpu.SemaphoreType.REGULAR((max(1, relays(zdim)),)),
         ],
         compiler_params=pltpu.CompilerParams(
             collective_id=0, has_side_effects=True, vmem_limit_bytes=32 * 1024 * 1024

time: 57.6 us -> 56.4 us (0.979)
  Pallas kernels: 54.8 us -> 53.6 us
    pallas_call x1, Pallas kernels: 54.8 us -> 53.6 us  [body(): pl.pallas_call(functools.partial(kernel, sizes), out_shape=(jax.ShapeDtyp...]
where the time goes in v3:
time: 56.4 us; the launch traced here: 56.2 us
  Pallas kernels  53.6 us (95%)
  local copies, waits for them, and re-layouts  1.35 us (2%)
  between operations  1.29 us (2%)
    pallas_call x1, Pallas kernels, body(): pl.pallas_call(functools.partial(kernel, sizes), out_shape=(jax.ShapeDtyp...  53.6 us
    unnamed x2, local copies, waits for them, and re-layouts  1.35 us

profile of v3, /device:TPU:1, one launch (start us, length us, event | category | flops | bytes accessed | tf_op | source)
XLA Modules:
  0.0 56.2 jit_solution(12285531934615646470)
XLA Ops:
  1.3 53.6 %coding_window.1 = (bf16[12,48,256]{2,1,0:T(8,128)(2,1)S(1)}, f32[24,864]{1,0:T(8,128)S(1)}) custom-call(bf16[48,32,128]{2,1,0:T(8,128)(2,1)} %bitcast.6, bf16[96,432]{1,0:T(8,128)(2,1)} %w_in_hbm.1, f32[1,48]{1,0:T(1,128)} %bitcast.8, bf16[96,864]{1,0:T(8,128)(2,1)} %w_ent_hbm.1, s32[1,12]{1,0:T(1,128)} %bitcast.9, s32[1,1,1]{2,1,0:T(1,128)S(6)} %copy.11.count_hbm, ...), custom_call_target="tpu_custom_call" | custom-call | flops 1700000000 | bytes 1500000 | tf_op jit(solution)/shard_map/coding_window/pallas_call | solution.py:404
  54.9 0.7 %copy.12 = bf16[1,1,1,12,48,256]{5,4,3,2,1,0:T(8,128)(2,1)} copy(bf16[1,1,1,12,48,256]{5,4,3,2,1,0:T(8,128)(2,1)S(1)} %bitcast.5) | data formatting | bytes 589824
  55.6 0.6 %copy.13 = f32[24,864]{1,0:T(8,128)} copy(f32[24,864]{1,0:T(8,128)S(1)} %get-tuple-element.9) | data formatting | bytes 165888

commit v4 on v3

--- a/solution.py
+++ b/solution.py
@@ -12,11 +12,15 @@
 MESH = pl.DeviceIdType.MESH
 
 
-REACH = 3
-
-
-def relays(size):
-    return max(0, -(-(size // 2) // REACH) - 1)
+NEAR = 2
+
+
+def relay_strides(size):
+    strides, known = [], NEAR
+    while known < size // 2:
+        strides.append(known)
+        known *= 2
+    return strides
 
 
 def swap_blocks(parts, lane):
@@ -47,7 +51,7 @@
     x_hbm, w_in_hbm, bias_hbm, w_ent_hbm, tiles_hbm, count_hbm, cot_hbm,
     lat_ref, grad_ref,
     w_in_ref, bias_ref, w_ent_ref, tiles_ref, count_ref,
-    xv, xf, xb, cotv, frame_rows, edge_rows, halo, conv_in, state, ctx_out, ctx, ctx_edge,
+    xv, xf, xb, cotv, frame_rows, edge_rows, halo, conv_in, gates, drives, state, ctx_out, ctx, ctx_edge,
     w_part, pre_x, joined, cot_dense, push, lat_dense, lat_tiles, grad_all, pieces, parts, z_in, final,
     load_sem, main_send, main_recv, edge_send, edge_recv, halo_send, halo_recv,
     ctx_send, ctx_recv, ctx_edge_send, ctx_edge_recv,
@@ -62,7 +66,7 @@
     plane = ydim * tdim
     spot = y * tdim + t
     per = 32 // tdim
-    rounds = relays(zdim)
+    strides = relay_strides(zdim)
     out_rows = 96 // ydim
     pend = []
 
@@ -95,24 +99,16 @@
 
     barrier = pltpu.get_barrier_semaphore()
 
-    @pl.loop(1, plane)
-    def _(d):
-        peer = lax.rem(spot + d, plane)
-        pl.semaphore_signal(
-            barrier, inc=1, device_id={"dp": peer // tdim, "tm": lax.rem(peer, tdim)}, device_id_type=MESH
-        )
-
-    @pl.loop(0, tdim)
-    def _(d):
-        pl.semaphore_signal(barrier, inc=1, device_id={"tm": d, "tile": above}, device_id_type=MESH)
-        pl.semaphore_signal(barrier, inc=1, device_id={"tm": d, "tile": below}, device_id_type=MESH)
-
-    greeted = plane - 1 + 2 * tdim
-    for d in range(2, zdim - 1):
-        if min(d, zdim - d) > REACH:
-            continue
-        pl.semaphore_signal(barrier, inc=1, device_id={"tile": lax.rem(b + d, zdim)}, device_id_type=MESH)
-        greeted += 1
+    greeted = 0
+    for axis, size, offsets in (
+        ("tm", tdim, range(1, tdim)),
+        ("tile", zdim, [d for d in range(1, zdim) if min(d, zdim - d) <= NEAR]),
+        ("dp", ydim, range(1, ydim)),
+    ):
+        for d in offsets:
+            peer = lax.rem(lax.axis_index(axis) + d, size)
+            pl.semaphore_signal(barrier, inc=1, device_id={axis: peer}, device_id_type=MESH)
+            greeted += 1
 
     lane = lax.broadcasted_iota(jnp.int32, (48, 128), 1)
     blank = jnp.zeros((48, 128), BF)
@@ -126,29 +122,26 @@
 
     pl.semaphore_wait(barrier, greeted)
 
-    def relay(step):
-        for d in (REACH, zdim - REACH):
-            pl.semaphore_signal(
-                relay_sem.at[step], inc=1, device_id={"tile": lax.rem(b + d, zdim)}, device_id_type=MESH
-            )
-
-    if rounds > 0:
-        relay(0)
+    def relay(step, axis, size, offsets):
+        for d in offsets:
+            peer = lax.rem(lax.axis_index(axis) + d, size)
+            pl.semaphore_signal(relay_sem.at[step], inc=1, device_id={axis: peer}, device_id_type=MESH)
 
     sends = t < tdim - 1
-    send(sends, lambda: remote(xb.at[32], edge_rows.at[t], edge_send.at[0], edge_recv.at[t], tm=0, tile=below))
-    send(sends, lambda: remote(xb.at[1], edge_rows.at[t], edge_send.at[1], edge_recv.at[t], tm=tdim - 1, tile=above))
+    always = t >= 0
+    send(always, lambda: remote(xb.at[32], halo.at[0], halo_send.at[0], halo_recv.at[0], tile=below))
+    send(always, lambda: remote(xb.at[1], halo.at[1], halo_send.at[1], halo_recv.at[1], tile=above))
     for d in range(1, tdim):
-        j = lax.rem(t + d, tdim)
+        j = lax.rem(t + tdim - d, tdim)
         send(
             sends,
             lambda d=d, j=j: remote(
                 xb.at[pl.ds(per * j, per + 2)], frame_rows.at[t], main_send.at[d], main_recv.at[t], tm=j
             ),
         )
-    always = t >= 0
-    send(always, lambda: remote(xb.at[32], halo.at[0], halo_send.at[0], halo_recv.at[0], tile=below))
-    send(always, lambda: remote(xb.at[1], halo.at[1], halo_send.at[1], halo_recv.at[1], tile=above))
+    relay(len(strides), "dp", ydim, range(1, ydim))
+    if strides:
+        relay(0, "tile", zdim, (strides[0], zdim - strides[0]))
 
     @pl.when(sends)
     def _():
@@ -179,7 +172,18 @@
 
     for edge, row, there in ((0, 0, b > 0), (1, 33, b < zdim - 1)):
         arrived(halo.at[edge], halo_recv.at[edge])
+        end = edge * (tdim - 1)
+        send(
+            sends & (t != end),
+            lambda edge=edge, end=end: remote(
+                halo.at[edge], edge_rows.at[t], edge_send.at[edge], edge_recv.at[t], tm=end
+            ),
+        )
         store_shifts(joined, 288 * row, 96, jnp.where(there, halo[edge], blank), lane)
+
+    @pl.when(t == 0)
+    def _():
+        edge_rows[0] = halo[0]
 
     loads[6].wait()
     w_all = w_ent_ref[...]
@@ -194,37 +198,38 @@
         cells = jnp.concatenate([taps(0, 16 * block + r) for r in range(16)], axis=1)
         pre_x[block] = jnp.dot(w_part[0], cells, preferred_element_type=F32)
 
-    for step in range(1, rounds):
+    for step in range(1, len(strides)):
         pl.semaphore_wait(relay_sem.at[step - 1], 2)
-        relay(step)
+        relay(step, "tile", zdim, (strides[step], zdim - strides[step]))
 
     state[...] = jnp.zeros_like(state)
     for load in loads[4:6]:
         load.wait()
     bias = bias_ref[...].T[:48, :1]
 
-    @pl.loop(0, tdim - 1)
-    def _(f):
+    def convolve(f):
         @pl.when(t != f)
         def _():
             arrived(frame_rows.at[f], main_recv.at[f])
 
-        @pl.when(t == 0)
-        def _():
-            arrived(edge_rows.at[f], edge_recv.at[f])
-            frame_rows[f, 0] = jnp.where(b > 0, edge_rows[f], blank)
-
-        @pl.when(t == tdim - 1)
-        def _():
-            arrived(edge_rows.at[f], edge_recv.at[f])
-            frame_rows[f, per + 1] = jnp.where(b < zdim - 1, edge_rows[f], blank)
+        for end, row, there in ((0, 0, b > 0), (tdim - 1, per + 1, b < zdim - 1)):
+            @pl.when(t == end)
+            def _():
+                @pl.when(f != end)
+                def _():
+                    arrived(edge_rows.at[f], edge_recv.at[f])
+
+                frame_rows[f, row] = jnp.where(there, edge_rows[f], blank)
 
         for r in range(per + 2):
             store_shifts(conv_in, 144 * r, 48, frame_rows[f, r], lane)
         cells = jnp.concatenate([conv_in[pl.ds(144 * r, 432), :] for r in range(per)], axis=1)
         mixed = jnp.dot(w_in_ref[...], cells, preferred_element_type=F32)
-        gate = 0.5 * jnp.tanh(0.5 * (mixed[:48] + bias)) + 0.5
-        now = gate * state[...] + jnp.tanh(mixed[48:])
+        gates[f] = 0.5 * jnp.tanh(0.5 * (mixed[:48] + bias)) + 0.5
+        drives[f] = jnp.tanh(mixed[48:])
+
+    def advance(f):
+        now = gates[f] * state[...] + drives[f]
         state[...] = now
         for r in range(per):
             ctx_out[f, r] = now[:, 128 * r : 128 * r + 128].astype(BF)
@@ -253,8 +258,28 @@
                 tm=f + 1, tile=above,
             ).start()
 
-    if rounds > 0:
-        pl.semaphore_wait(relay_sem.at[rounds - 1], 2)
+    @pl.loop(0, tdim)
+    def _(i):
+        f = lax.rem(t + i, tdim)
+
+        @pl.when(f < tdim - 1)
+        def _():
+            convolve(f)
+
+            @pl.when((f < t) | (t == 0))
+            def _():
+                advance(f)
+
+    @pl.loop(0, tdim - 1)
+    def _(f):
+        @pl.when((f >= t) & (t > 0))
+        def _():
+            advance(f)
+
+    if strides:
+        pl.semaphore_wait(relay_sem.at[len(strides) - 1], 2)
+    if ydim > 1:
+        pl.semaphore_wait(relay_sem.at[len(strides)], ydim - 1)
 
     @pl.when(t == 0)
     def _():
@@ -295,33 +320,44 @@
             push[96 * (33 - r) : 96 * (33 - r) + 48, :] = near.astype(BF)
             push[96 * (33 - r) + 48 : 96 * (34 - r), :] = (near * lat * slope).astype(BF)
 
-    for first, last in ((0, 18), (18, 34)):
-        near = jnp.concatenate([push[96 * (33 - r) : 96 * (36 - r), :] for r in range(first, last)], axis=1)
-        rows = jnp.concatenate([joined[288 * r : 288 * r + 288, :] for r in range(first, last)], axis=1)
-        term = lax.dot_general(near, rows, (((1,), (1,)), ((), ())), preferred_element_type=F32)
-        if first == 0:
-            grad_all[...] = term
-        else:
-            grad_all[...] += term
-
+    near = jnp.concatenate([push[96 * (33 - r) : 96 * (36 - r), :] for r in range(34)], axis=1)
+
+    def gradient(first, last):
+        rows = jnp.concatenate([joined[288 * r + first : 288 * r + last, :] for r in range(34)], axis=1)
+        return lax.dot_general(near, rows, (((1,), (1,)), ((), ())), preferred_element_type=F32)
+
+    def send_piece(other, l):
+        remote(pieces.at[7 * other + l], parts.at[spot], piece_send, piece_recv, dp=other, tm=l).start()
+
+    grad_all[...] = gradient(0, 256)
     for other in range(ydim):
-        tails = []
         for dy in range(3):
             block = grad_all[96 * dy + out_rows * other : 96 * dy + out_rows * (other + 1), :]
             pieces[7 * other + 2 * dy, :out_rows] = block[:, :128].astype(BF)
-            pieces[7 * other + 2 * dy + 1, :out_rows] = block[:, 128:256].astype(BF)
-            tails.append(block[:, 256:])
-        tails.append(jnp.zeros_like(tails[0]))
-        pieces[7 * other + 6, :out_rows] = jnp.concatenate(tails, axis=1).astype(BF)
+            pieces[7 * other + 2 * dy + 1, :out_rows] = block[:, 128:].astype(BF)
 
     @pl.loop(1, plane)
     def _(d):
         peer = lax.rem(spot + d, plane)
         other, l = peer // tdim, lax.rem(peer, tdim)
 
-        @pl.when(l < 7)
-        def _():
-            remote(pieces.at[7 * other + l], parts.at[spot], piece_send, piece_recv, dp=other, tm=l).start()
+        @pl.when(l < 6)
+        def _():
+            send_piece(other, l)
+
+    grad_all[:, :32] = gradient(256, 288)
+    for other in range(ydim):
+        tails = [grad_all[96 * dy + out_rows * other : 96 * dy + out_rows * (other + 1), :32] for dy in range(3)]
+        tails.append(jnp.zeros_like(tails[0]))
+        pieces[7 * other + 6, :out_rows] = jnp.concatenate(tails, axis=1).astype(BF)
+
+    @pl.loop(0, ydim)
+    def _(d):
+        other = lax.rem(y + d, ydim)
+
+        @pl.when((t != 6) | (d > 0))
+        def _():
+            send_piece(other, 6)
 
     for half in range(2):
         for h in range(2):
@@ -423,6 +459,8 @@
             pltpu.VMEM((tdim, 48, 128), BF),
             pltpu.VMEM((2, 48, 128), BF),
             pltpu.VMEM(((per + 2) * 144, 128), BF),
+            pltpu.VMEM((tdim - 1, 48, per * 128), F32),
+            pltpu.VMEM((tdim - 1, 48, per * 128), F32),
             pltpu.VMEM((48, per * 128), F32),
             pltpu.VMEM((tdim - 1, per, 48, 128), BF),
             pltpu.VMEM((34, 48, 128), BF),
@@ -434,7 +472,7 @@
             pltpu.VMEM((36 * 96, 128), BF),
             pltpu.VMEM((32, 48, 128), F32),
             pltpu.VMEM((16, 48, 256), BF),
-            pltpu.VMEM((288, 288), F32),
+            pltpu.VMEM((288, 256), F32),
             pltpu.VMEM((7 * ydim, held_rows, 128), BF),
             pltpu.VMEM((plane, held_rows, 128), BF),
             pltpu.VMEM((zdim, held_rows, 128), BF),
@@ -448,7 +486,7 @@
             dma, dma,
             dma((zdim,)), dma,
             dma((tdim - 1,)), dma((7,)),
-            pltpu.SemaphoreType.REGULAR((max(1, relays(zdim)),)),
+            pltpu.SemaphoreType.REGULAR((len(relay_strides(zdim)) + 1,)),
         ],
         compiler_params=pltpu.CompilerParams(
             collective_id=0, has_side_effects=True, vmem_limit_bytes=32 * 1024 * 1024

time: 56.4 us -> 54.5 us (0.966)
  Pallas kernels: 53.6 us -> 51.8 us
    pallas_call x1, Pallas kernels: 53.6 us -> 51.8 us  [body(): pl.pallas_call(functools.partial(kernel, sizes), out_shape=(jax.ShapeDtyp...]
where the time goes in v4:
time: 54.5 us; the launch traced here: 54.4 us
  Pallas kernels  51.8 us (95%)
  local copies, waits for them, and re-layouts  1.35 us (2%)
  between operations  1.29 us (2%)
    pallas_call x1, Pallas kernels, body(): pl.pallas_call(functools.partial(kernel, sizes), out_shape=(jax.ShapeDtyp...  51.8 us
    unnamed x2, local copies, waits for them, and re-layouts  1.35 us

profile of v4, /device:TPU:1, one launch (start us, length us, event | category | flops | bytes accessed | tf_op | source)
XLA Modules:
  0.0 54.4 jit_solution(12831087955494836338)
XLA Ops:
  1.3 51.8 %coding_window.1 = (bf16[12,48,256]{2,1,0:T(8,128)(2,1)S(1)}, f32[24,864]{1,0:T(8,128)S(1)}) custom-call(bf16[48,32,128]{2,1,0:T(8,128)(2,1)} %bitcast.6, bf16[96,432]{1,0:T(8,128)(2,1)} %w_in_hbm.1, f32[1,48]{1,0:T(1,128)} %bitcast.8, bf16[96,864]{1,0:T(8,128)(2,1)} %w_ent_hbm.1, s32[1,12]{1,0:T(1,128)} %bitcast.9, s32[1,1,1]{2,1,0:T(1,128)S(6)} %copy.11.count_hbm, ...), custom_call_target="tpu_custom_call" | custom-call | flops 1700000000 | bytes 1500000 | tf_op jit(solution)/shard_map/coding_window/pallas_call | solution.py:440
  53.0 0.7 %copy.12 = bf16[1,1,1,12,48,256]{5,4,3,2,1,0:T(8,128)(2,1)} copy(bf16[1,1,1,12,48,256]{5,4,3,2,1,0:T(8,128)(2,1)S(1)} %bitcast.5) | data formatting | bytes 589824
  53.8 0.6 %copy.13 = f32[24,864]{1,0:T(8,128)} copy(f32[24,864]{1,0:T(8,128)S(1)} %get-tuple-element.9) | data formatting | bytes 165888

commit v5 on v4

--- a/solution.py
+++ b/solution.py
@@ -336,14 +336,17 @@
             pieces[7 * other + 2 * dy, :out_rows] = block[:, :128].astype(BF)
             pieces[7 * other + 2 * dy + 1, :out_rows] = block[:, 128:].astype(BF)
 
-    @pl.loop(1, plane)
-    def _(d):
-        peer = lax.rem(spot + d, plane)
-        other, l = peer // tdim, lax.rem(peer, tdim)
+    def hops(way):
+        dy, dt = way
+        return min(dy, ydim - dy) + min(dt // 2, (tdim - dt) // 2)
+
+    ways = [(dy, dt) for dy in range(ydim) for dt in range(tdim) if dy + dt > 0]
+    for dy, dt in sorted(ways, key=hops, reverse=True):
+        l = lax.rem(t + dt, tdim)
 
         @pl.when(l < 6)
-        def _():
-            send_piece(other, l)
+        def _(dy=dy, l=l):
+            send_piece(lax.rem(y + dy, ydim), l)
 
     grad_all[:, :32] = gradient(256, 288)
     for other in range(ydim):
@@ -369,6 +372,21 @@
         lat_ref[k] = jnp.where(k < count, held, jnp.zeros_like(held))
 
     owner = t < 7
+
+    for cond, make in pend:
+        @pl.when(cond)
+        def _(make=make):
+            make().wait_send()
+
+    @pl.loop(0, tdim - 1)
+    def _(f):
+        @pl.when(t != f + 1)
+        def _():
+            arrived(ctx_out.at[f], ctx_send.at[f])
+
+        @pl.when((t == 0) | (t == tdim - 1))
+        def _():
+            arrived(ctx_out.at[f, 0], ctx_edge_send.at[f])
 
     @pl.when(owner)
     def _():
@@ -390,6 +408,16 @@
                 final.at[t], final.at[t], final_send.at[d - 1], final_recv.at[t], tm=lax.rem(t + d, tdim)
             ).start()
 
+    @pl.when(owner)
+    def _():
+        arrived(pieces.at[pl.ds(0, 7 * ydim - 1)], piece_send)
+        for d in range(1, zdim):
+            arrived(z_in.at[b], z_send.at[d])
+
+    @pl.when(t == tdim - 1)
+    def _():
+        arrived(pieces, piece_send)
+
     for l in range(7):
         @pl.when(t != l)
         def _():
@@ -400,32 +428,21 @@
             [final[2 * dy], final[2 * dy + 1], final[6][:, 32 * dy : 32 * (dy + 1)]], axis=1
         )
 
-    for cond, make in pend:
-        @pl.when(cond)
-        def _(make=make):
-            make().wait_send()
-
-    @pl.loop(0, tdim - 1)
-    def _(f):
-        @pl.when(t != f + 1)
-        def _():
-            arrived(ctx_out.at[f], ctx_send.at[f])
-
-        @pl.when((t == 0) | (t == tdim - 1))
-        def _():
-            arrived(ctx_out.at[f, 0], ctx_edge_send.at[f])
-
     @pl.when(owner)
     def _():
-        arrived(pieces.at[pl.ds(0, 7 * ydim - 1)], piece_send)
-        for d in range(1, zdim):
-            arrived(z_in.at[b], z_send.at[d])
         for d in range(1, tdim):
             arrived(final.at[t], final_send.at[d - 1])
 
-    @pl.when(t == tdim - 1)
-    def _():
-        arrived(pieces, piece_send)
+
+def store_kernel(lat_ref, grad_ref, lat_hbm, grad_hbm, sem):
+    copies = [
+        pltpu.make_async_copy(lat_ref, lat_hbm, sem.at[0]),
+        pltpu.make_async_copy(grad_ref, grad_hbm, sem.at[1]),
+    ]
+    for copy in copies:
+        copy.start()
+    for copy in copies:
+        copy.wait()
 
 
 def body(sizes, frames_in, w_in, gate_bias, w_ent, active_tiles, active_count, cotangent):
@@ -502,6 +519,19 @@
         active_count,
         pltpu.with_memory_space_constraint(cotangent[0, 0, 0], pltpu.HBM),
     )
+    anywhere = pl.BlockSpec(memory_space=pl.ANY)
+    latent, grad = pl.pallas_call(
+        store_kernel,
+        out_shape=(
+            jax.ShapeDtypeStruct((12, 48, 256), BF),
+            jax.ShapeDtypeStruct((out_rows, 864), F32),
+        ),
+        in_specs=[anywhere] * 2,
+        out_specs=(anywhere,) * 2,
+        scratch_shapes=[dma((2,))],
+        cost_estimate=pl.CostEstimate(flops=0, bytes_accessed=800_000, transcendentals=0),
+        name="store_outputs",
+    )(latent, grad)
     return (latent[None, None, None], grad)
 
 

time: 54.5 us -> 66.9 us (1.23)
  Pallas kernels: 51.8 us -> 64.1 us
    pallas_call x0 -> x1, Pallas kernels: none -> 12.7 us  [body(): pl.pallas_call(store_kernel, out_shape=(jax.ShapeDtypeStruct((12, 48, 256...]
    unnamed x2 -> x4, local copies, waits for them, and re-layouts: 1.35 us -> 1.34 us
where the time goes in v5:
time: 66.9 us; the launch traced here: 66.8 us
  Pallas kernels  64.1 us (96%)
  local copies, waits for them, and re-layouts  1.34 us (2%)
  between operations  1.3 us (2%)
    pallas_call x1, Pallas kernels, body(): pl.pallas_call(functools.partial(kernel, sizes), out_shape=(jax.ShapeDtyp...  51.5 us
    pallas_call x1, Pallas kernels, body(): pl.pallas_call(store_kernel, out_shape=(jax.ShapeDtypeStruct((12, 48, 256...  12.7 us
    unnamed x4, local copies, waits for them, and re-layouts  1.34 us

profile of v5, /device:TPU:1, one launch (start us, length us, event | category | flops | bytes accessed | tf_op | source)
XLA Modules:
  0.0 66.8 jit_solution(17439438933782837760)
XLA Ops:
  1.3 51.5 %coding_window.1 = (bf16[12,48,256]{2,1,0:T(8,128)(2,1)S(1)}, f32[24,864]{1,0:T(8,128)S(1)}) custom-call(bf16[48,32,128]{2,1,0:T(8,128)(2,1)} %bitcast.5, bf16[96,432]{1,0:T(8,128)(2,1)} %w_in_hbm.1, f32[1,48]{1,0:T(1,128)} %bitcast.8, bf16[96,864]{1,0:T(8,128)(2,1)} %w_ent_hbm.1, s32[1,12]{1,0:T(1,128)} %bitcast.9, s32[1,1,1]{2,1,0:T(1,128)S(6)} %copy.9.count_hbm, ...), custom_call_target="tpu_custom_call" | custom-call | flops 1700000000 | bytes 1500000 | tf_op jit(solution)/shard_map/coding_window/pallas_call | solution.py:457
  52.8 0.0 copy-start
  52.8 0.7 %copy-done = bf16[12,48,256]{2,1,0:T(8,128)(2,1)} copy-done((bf16[12,48,256]{2,1,0:T(8,128)(2,1)}, bf16[12,48,256]{2,1,0:T(8,128)(2,1)S(1)}, u32[]{:S(2)}) %copy-start) | copy-done | bytes 294936
  53.5 0.0 copy-start.1
  53.5 0.6 copy-done.1
  54.1 12.7 %store_outputs.1 = (bf16[12,48,256]{2,1,0:T(8,128)(2,1)}, f32[24,864]{1,0:T(8,128)}) custom-call(bf16[12,48,256]{2,1,0:T(8,128)(2,1)} %copy-done, f32[24,864]{1,0:T(8,128)} %copy-done.1), custom_call_target="tpu_custom_call" | custom-call | bytes 800000 | tf_op jit(solution)/shard_map/store_outputs/pallas_call | solution.py:523
Async XLA Ops:
  52.8 0.7 %copy-start = (bf16[12,48,256]{2,1,0:T(8,128)(2,1)}, bf16[12,48,256]{2,1,0:T(8,128)(2,1)S(1)}, u32[]{:S(2)}) copy-start(bf16[12,48,256]{2,1,0:T(8,128)(2,1)S(1)} %get-tuple-element.6.lat_ref) | copy-start | bytes 884740
  53.5 0.6 copy-start.1

commit v6 on v4

--- a/solution.py
+++ b/solution.py
@@ -21,6 +21,13 @@
         strides.append(known)
         known *= 2
     return strides
+
+
+def shares(out_rows):
+    first, last = 6 * out_rows // 16, -(-out_rows // 16)
+    return [16 * (first * (i + 1) // 6 - first * i // 6) for i in range(6)] + [
+        16 * (last * (i + 1) // 2 - last * i // 2) for i in range(2)
+    ]
 
 
 def swap_blocks(parts, lane):
@@ -68,6 +75,8 @@
     per = 32 // tdim
     strides = relay_strides(zdim)
     out_rows = 96 // ydim
+    shared = shares(out_rows)
+    block_rows = sum(shared)
     pend = []
 
     def send(cond, make):
@@ -326,38 +335,52 @@
         rows = jnp.concatenate([joined[288 * r + first : 288 * r + last, :] for r in range(34)], axis=1)
         return lax.dot_general(near, rows, (((1,), (1,)), ((), ())), preferred_element_type=F32)
 
-    def send_piece(other, l):
-        remote(pieces.at[7 * other + l], parts.at[spot], piece_send, piece_recv, dp=other, tm=l).start()
+    def owned_from(l):
+        return pl.multiple_of(sum(shared[k] * ((l + 7 - k) // 8) for k in range(7)), 16)
+
+    def sized(l, among):
+        for size in sorted({shared[k] for k in among}):
+            has = l < 0
+            for k in among:
+                if shared[k] == size:
+                    has = has | (l == k)
+            yield size, has
+
+    def send_piece(other, l, size):
+        src = pieces.at[pl.ds(block_rows * other + owned_from(l), size)]
+        remote(src, parts.at[spot, pl.ds(0, size)], piece_send, piece_recv, dp=other, tm=l).start()
+
+    def hops(way):
+        dy, dt = way
+        return min(dy, ydim - dy) + min(dt // 2, (tdim - dt) // 2)
+
+    ways = [(dy, dt) for dy in range(ydim) for dt in range(tdim) if dy + dt > 0]
+    ways = sorted(ways, key=hops, reverse=True)
+
+    def send_pieces(among):
+        for dy, dt in ways:
+            l = lax.rem(t + dt, tdim)
+            for size, has in sized(l, among):
+                @pl.when(has)
+                def _(dy=dy, l=l, size=size):
+                    send_piece(lax.rem(y + dy, ydim), l, size)
 
     grad_all[...] = gradient(0, 256)
     for other in range(ydim):
         for dy in range(3):
             block = grad_all[96 * dy + out_rows * other : 96 * dy + out_rows * (other + 1), :]
-            pieces[7 * other + 2 * dy, :out_rows] = block[:, :128].astype(BF)
-            pieces[7 * other + 2 * dy + 1, :out_rows] = block[:, 128:].astype(BF)
-
-    @pl.loop(1, plane)
-    def _(d):
-        peer = lax.rem(spot + d, plane)
-        other, l = peer // tdim, lax.rem(peer, tdim)
-
-        @pl.when(l < 6)
-        def _():
-            send_piece(other, l)
+            for half in range(2):
+                start = block_rows * other + out_rows * (3 * half + dy)
+                pieces[start : start + out_rows, :] = block[:, 128 * half : 128 * half + 128].astype(BF)
+    send_pieces(range(6))
 
     grad_all[:, :32] = gradient(256, 288)
     for other in range(ydim):
         tails = [grad_all[96 * dy + out_rows * other : 96 * dy + out_rows * (other + 1), :32] for dy in range(3)]
         tails.append(jnp.zeros_like(tails[0]))
-        pieces[7 * other + 6, :out_rows] = jnp.concatenate(tails, axis=1).astype(BF)
-
-    @pl.loop(0, ydim)
-    def _(d):
-        other = lax.rem(y + d, ydim)
-
-        @pl.when((t != 6) | (d > 0))
-        def _():
-            send_piece(other, 6)
+        start = block_rows * other + 6 * out_rows
+        pieces[start : start + out_rows, :] = jnp.concatenate(tails, axis=1).astype(BF)
+    send_pieces(range(6, 8))
 
     for half in range(2):
         for h in range(2):
@@ -368,38 +391,6 @@
         held = lat_tiles[tiles_ref[0, k]]
         lat_ref[k] = jnp.where(k < count, held, jnp.zeros_like(held))
 
-    owner = t < 7
-
-    @pl.when(owner)
-    def _():
-        parts[spot] = pieces[7 * y + t]
-        arrived(parts.at[pl.ds(0, plane - 1)], piece_recv)
-        total = parts[0].astype(F32)
-        for i in range(1, plane):
-            total = total + parts[i].astype(F32)
-        z_in[b] = total.astype(BF)
-        for d in sorted(range(1, zdim), key=lambda d: -min(d, zdim - d)):
-            remote(z_in.at[b], z_in.at[b], z_send.at[d], z_recv, tile=lax.rem(b + d, zdim)).start()
-        arrived(z_in.at[pl.ds(0, zdim - 1)], z_recv)
-        total = z_in[0].astype(F32)
-        for i in range(1, zdim):
-            total = total + z_in[i].astype(F32)
-        final[t] = total[:out_rows]
-        for d in range(1, tdim):
-            remote(
-                final.at[t], final.at[t], final_send.at[d - 1], final_recv.at[t], tm=lax.rem(t + d, tdim)
-            ).start()
-
-    for l in range(7):
-        @pl.when(t != l)
-        def _():
-            arrived(final.at[l], final_recv.at[l])
-
-    for dy in range(3):
-        grad_ref[:, 288 * dy : 288 * (dy + 1)] = jnp.concatenate(
-            [final[2 * dy], final[2 * dy + 1], final[6][:, 32 * dy : 32 * (dy + 1)]], axis=1
-        )
-
     for cond, make in pend:
         @pl.when(cond)
         def _(make=make):
@@ -415,17 +406,54 @@
         def _():
             arrived(ctx_out.at[f, 0], ctx_edge_send.at[f])
 
-    @pl.when(owner)
-    def _():
-        arrived(pieces.at[pl.ds(0, 7 * ydim - 1)], piece_send)
+    def add_up(size):
+        start = owned_from(t)
+        mine = pl.ds(start, size)
+        used = pl.ds(0, size)
+        parts[spot, used] = pieces[pl.ds(block_rows * y + start, size)]
+        arrived(parts.at[pl.ds(0, plane - 1), used], piece_recv)
+        total = parts[0, used].astype(F32)
+        for i in range(1, plane):
+            total = total + parts[i, used].astype(F32)
+        z_in[b, used] = total.astype(BF)
+        for d in sorted(range(1, zdim), key=lambda d: -min(d, zdim - d)):
+            remote(
+                z_in.at[b, used], z_in.at[b, used], z_send.at[d], z_recv, tile=lax.rem(b + d, zdim)
+            ).start()
+        arrived(pieces.at[pl.ds(0, block_rows * ydim - size)], piece_send)
+        arrived(z_in.at[pl.ds(0, zdim - 1), used], z_recv)
+        total = z_in[0, used].astype(F32)
+        for i in range(1, zdim):
+            total = total + z_in[i, used].astype(F32)
+        final[mine] = total
+        for d in range(1, tdim):
+            remote(
+                final.at[mine], final.at[mine], final_send.at[d - 1], final_recv.at[t], tm=lax.rem(t + d, tdim)
+            ).start()
         for d in range(1, zdim):
-            arrived(z_in.at[b], z_send.at[d])
-        for d in range(1, tdim):
-            arrived(final.at[t], final_send.at[d - 1])
-
-    @pl.when(t == tdim - 1)
-    def _():
-        arrived(pieces, piece_send)
+            arrived(z_in.at[b, used], z_send.at[d])
+
+    for size, has in sized(t, range(8)):
+        @pl.when(has)
+        def _(size=size):
+            add_up(size)
+
+    for l in range(8):
+        @pl.when(t != l)
+        def _():
+            arrived(final.at[pl.ds(sum(shared[:l]), shared[l])], final_recv.at[l])
+
+    for dy in range(3):
+        at = [out_rows * dy, out_rows * (3 + dy), out_rows * 6]
+        columns = [final[a : a + out_rows, :] for a in at]
+        columns[2] = columns[2][:, 32 * dy : 32 * (dy + 1)]
+        grad_ref[:, 288 * dy : 288 * (dy + 1)] = jnp.concatenate(columns, axis=1)
+
+    for size, has in sized(t, range(8)):
+        @pl.when(has)
+        def _(size=size):
+            for d in range(1, tdim):
+                arrived(final.at[pl.ds(0, size)], final_send.at[d - 1])
 
 
 def body(sizes, frames_in, w_in, gate_bias, w_ent, active_tiles, active_count, cotangent):
@@ -433,7 +461,7 @@
     plane = ydim * tdim
     per = 32 // tdim
     out_rows = 96 // ydim
-    held_rows = -(-out_rows // 16) * 16
+    shared = shares(out_rows)
     vmem = pl.BlockSpec(memory_space=pltpu.VMEM)
     hbm = pl.BlockSpec(memory_space=pltpu.HBM)
     dma = pltpu.SemaphoreType.DMA
@@ -473,10 +501,10 @@
             pltpu.VMEM((32, 48, 128), F32),
             pltpu.VMEM((16, 48, 256), BF),
             pltpu.VMEM((288, 256), F32),
-            pltpu.VMEM((7 * ydim, held_rows, 128), BF),
-            pltpu.VMEM((plane, held_rows, 128), BF),
-            pltpu.VMEM((zdim, held_rows, 128), BF),
-            pltpu.VMEM((7, out_rows, 128), F32),
+            pltpu.VMEM((ydim * sum(shared), 128), BF),
+            pltpu.VMEM((plane, max(shared), 128), BF),
+            pltpu.VMEM((zdim, max(shared), 128), BF),
+            pltpu.VMEM((sum(shared), 128), F32),
             dma((7,)),
             dma((tdim,)), dma((tdim,)),
             dma((2,)), dma((tdim,)),
@@ -485,7 +513,7 @@
             dma((tdim - 1,)), dma((2,)),
             dma, dma,
             dma((zdim,)), dma,
-            dma((tdim - 1,)), dma((7,)),
+            dma((tdim - 1,)), dma((tdim,)),
             pltpu.SemaphoreType.REGULAR((len(relay_strides(zdim)) + 1,)),
         ],
         compiler_params=pltpu.CompilerParams(

time: 54.5 us -> 54.1 us (level)
  no operation moved by 1% of the time
where the time goes in v6:
time: 54.1 us; the launch traced here: 53.9 us
  Pallas kernels  51.3 us (95%)
  local copies, waits for them, and re-layouts  1.35 us (2%)
  between operations  1.29 us (2%)
    pallas_call x1, Pallas kernels, body(): pl.pallas_call(functools.partial(kernel, sizes), out_shape=(jax.ShapeDtyp...  51.3 us
    unnamed x2, local copies, waits for them, and re-layouts  1.35 us

profile of v6, /device:TPU:1, one launch (start us, length us, event | category | flops | bytes accessed | tf_op | source)
XLA Modules:
  0.0 53.9 jit_solution(16624543751007117043)
XLA Ops:
  1.3 51.3 %coding_window.1 = (bf16[12,48,256]{2,1,0:T(8,128)(2,1)S(1)}, f32[24,864]{1,0:T(8,128)S(1)}) custom-call(bf16[48,32,128]{2,1,0:T(8,128)(2,1)} %bitcast.6, bf16[96,432]{1,0:T(8,128)(2,1)} %w_in_hbm.1, f32[1,48]{1,0:T(1,128)} %bitcast.8, bf16[96,864]{1,0:T(8,128)(2,1)} %w_ent_hbm.1, s32[1,12]{1,0:T(1,128)} %bitcast.9, s32[1,1,1]{2,1,0:T(1,128)S(6)} %copy.11.count_hbm, ...), custom_call_target="tpu_custom_call" | custom-call | flops 1700000000 | bytes 1500000 | tf_op jit(solution)/shard_map/coding_window/pallas_call | solution.py:468
  52.6 0.7 %copy.12 = bf16[1,1,1,12,48,256]{5,4,3,2,1,0:T(8,128)(2,1)} copy(bf16[1,1,1,12,48,256]{5,4,3,2,1,0:T(8,128)(2,1)S(1)} %bitcast.5) | data formatting | bytes 589824
  53.3 0.6 %copy.13 = f32[24,864]{1,0:T(8,128)} copy(f32[24,864]{1,0:T(8,128)S(1)} %get-tuple-element.9) | data formatting | bytes 165888

commit v7 on v6

--- a/solution.py
+++ b/solution.py
@@ -103,8 +103,7 @@
             )
         )
     ]
-    for load in loads:
-        load.start()
+    loads[0].start()
 
     barrier = pltpu.get_barrier_semaphore()
 
@@ -119,6 +118,8 @@
             pl.semaphore_signal(barrier, inc=1, device_id={axis: peer}, device_id_type=MESH)
             greeted += 1
 
+    for load in loads[1:]:
+        load.start()
     lane = lax.broadcasted_iota(jnp.int32, (48, 128), 1)
     blank = jnp.zeros((48, 128), BF)
 
@@ -350,20 +351,15 @@
         src = pieces.at[pl.ds(block_rows * other + owned_from(l), size)]
         remote(src, parts.at[spot, pl.ds(0, size)], piece_send, piece_recv, dp=other, tm=l).start()
 
-    def hops(way):
-        dy, dt = way
-        return min(dy, ydim - dy) + min(dt // 2, (tdim - dt) // 2)
-
-    ways = [(dy, dt) for dy in range(ydim) for dt in range(tdim) if dy + dt > 0]
-    ways = sorted(ways, key=hops, reverse=True)
-
     def send_pieces(among):
-        for dy, dt in ways:
-            l = lax.rem(t + dt, tdim)
-            for size, has in sized(l, among):
-                @pl.when(has)
-                def _(dy=dy, l=l, size=size):
-                    send_piece(lax.rem(y + dy, ydim), l, size)
+        for dy in sorted(range(ydim), key=lambda dy: -min(dy, ydim - dy)):
+            @pl.loop(0, tdim)
+            def _(i):
+                l = lax.rem(t + tdim // 2 + i, tdim)
+                for size, has in sized(l, among):
+                    @pl.when(has & (l != t) if dy == 0 else has)
+                    def _():
+                        send_piece(lax.rem(y + dy, ydim), l, size)
 
     grad_all[...] = gradient(0, 256)
     for other in range(ydim):
@@ -416,10 +412,14 @@
         for i in range(1, plane):
             total = total + parts[i, used].astype(F32)
         z_in[b, used] = total.astype(BF)
-        for d in sorted(range(1, zdim), key=lambda d: -min(d, zdim - d)):
+
+        @pl.loop(0, zdim - 1)
+        def _(i):
+            d = zdim // 2 + i // 2 - lax.rem(i, 2) * (2 * (i // 2) + 1)
             remote(
                 z_in.at[b, used], z_in.at[b, used], z_send.at[d], z_recv, tile=lax.rem(b + d, zdim)
             ).start()
+
         arrived(pieces.at[pl.ds(0, block_rows * ydim - size)], piece_send)
         arrived(z_in.at[pl.ds(0, zdim - 1), used], z_recv)
         total = z_in[0, used].astype(F32)
@@ -430,7 +430,9 @@
             remote(
                 final.at[mine], final.at[mine], final_send.at[d - 1], final_recv.at[t], tm=lax.rem(t + d, tdim)
             ).start()
-        for d in range(1, zdim):
+
+        @pl.loop(1, zdim)
+        def _(d):
             arrived(z_in.at[b, used], z_send.at[d])
 
     for size, has in sized(t, range(8)):

time: 54.1 us -> 54.3 us (level)
  no operation moved by 1% of the time
where the time goes in v7:
time: 54.3 us; the launch traced here: 54.1 us
  Pallas kernels  51.5 us (95%)
  local copies, waits for them, and re-layouts  1.35 us (2%)
  between operations  1.29 us (2%)
    pallas_call x1, Pallas kernels, body(): pl.pallas_call(functools.partial(kernel, sizes), out_shape=(jax.ShapeDtyp...  51.5 us
    unnamed x2, local copies, waits for them, and re-layouts  1.35 us

profile of v7, /device:TPU:1, one launch (start us, length us, event | category | flops | bytes accessed | tf_op | source)
XLA Modules:
  0.0 54.1 jit_solution(9899806188782692897)
XLA Ops:
  1.3 51.5 %coding_window.1 = (bf16[12,48,256]{2,1,0:T(8,128)(2,1)S(1)}, f32[24,864]{1,0:T(8,128)S(1)}) custom-call(bf16[48,32,128]{2,1,0:T(8,128)(2,1)} %bitcast.6, bf16[96,432]{1,0:T(8,128)(2,1)} %w_in_hbm.1, f32[1,48]{1,0:T(1,128)} %bitcast.8, bf16[96,864]{1,0:T(8,128)(2,1)} %w_ent_hbm.1, s32[1,12]{1,0:T(1,128)} %bitcast.9, s32[1,1,1]{2,1,0:T(1,128)S(6)} %copy.11.count_hbm, ...), custom_call_target="tpu_custom_call" | custom-call | flops 1700000000 | bytes 1500000 | tf_op jit(solution)/shard_map/coding_window/pallas_call | solution.py:470
  52.8 0.7 %copy.12 = bf16[1,1,1,12,48,256]{5,4,3,2,1,0:T(8,128)(2,1)} copy(bf16[1,1,1,12,48,256]{5,4,3,2,1,0:T(8,128)(2,1)S(1)} %bitcast.5) | data formatting | bytes 589824
  53.5 0.6 %copy.13 = f32[24,864]{1,0:T(8,128)} copy(f32[24,864]{1,0:T(8,128)S(1)} %get-tuple-element.9) | data formatting | bytes 165888

commit v8 on v6

--- a/solution.py
+++ b/solution.py
@@ -103,8 +103,7 @@
             )
         )
     ]
-    for load in loads:
-        load.start()
+    loads[0].start()
 
     barrier = pltpu.get_barrier_semaphore()
 
@@ -119,6 +118,8 @@
             pl.semaphore_signal(barrier, inc=1, device_id={axis: peer}, device_id_type=MESH)
             greeted += 1
 
+    for load in loads[1:]:
+        load.start()
     lane = lax.broadcasted_iota(jnp.int32, (48, 128), 1)
     blank = jnp.zeros((48, 128), BF)
 
@@ -425,7 +426,7 @@
         total = z_in[0, used].astype(F32)
         for i in range(1, zdim):
             total = total + z_in[i, used].astype(F32)
-        final[mine] = total
+        final[mine] = total.astype(BF)
         for d in range(1, tdim):
             remote(
                 final.at[mine], final.at[mine], final_send.at[d - 1], final_recv.at[t], tm=lax.rem(t + d, tdim)
@@ -443,9 +444,10 @@
         def _():
             arrived(final.at[pl.ds(sum(shared[:l]), shared[l])], final_recv.at[l])
 
+    whole = final[...].astype(F32)
     for dy in range(3):
         at = [out_rows * dy, out_rows * (3 + dy), out_rows * 6]
-        columns = [final[a : a + out_rows, :] for a in at]
+        columns = [whole[a : a + out_rows, :] for a in at]
         columns[2] = columns[2][:, 32 * dy : 32 * (dy + 1)]
         grad_ref[:, 288 * dy : 288 * (dy + 1)] = jnp.concatenate(columns, axis=1)
 
@@ -504,7 +506,7 @@
             pltpu.VMEM((ydim * sum(shared), 128), BF),
             pltpu.VMEM((plane, max(shared), 128), BF),
             pltpu.VMEM((zdim, max(shared), 128), BF),
-            pltpu.VMEM((sum(shared), 128), F32),
+            pltpu.VMEM((sum(shared), 128), BF),
             dma((7,)),
             dma((tdim,)), dma((tdim,)),
             dma((2,)), dma((tdim,)),

time: 54.1 us -> 54 us (level)
  no operation moved by 1% of the time
where the time goes in v8:
time: 54 us; the launch traced here: 53.9 us
  Pallas kernels  51.2 us (95%)
  local copies, waits for them, and re-layouts  1.35 us (2%)
  between operations  1.29 us (2%)
    pallas_call x1, Pallas kernels, body(): pl.pallas_call(functools.partial(kernel, sizes), out_shape=(jax.ShapeDtyp...  51.2 us
    unnamed x2, local copies, waits for them, and re-layouts  1.35 us

profile of v8, /device:TPU:1, one launch (start us, length us, event | category | flops | bytes accessed | tf_op | source)
XLA Modules:
  0.0 53.9 jit_solution(9120849929616221459)
XLA Ops:
  1.3 51.2 %coding_window.1 = (bf16[12,48,256]{2,1,0:T(8,128)(2,1)S(1)}, f32[24,864]{1,0:T(8,128)S(1)}) custom-call(bf16[48,32,128]{2,1,0:T(8,128)(2,1)} %bitcast.6, bf16[96,432]{1,0:T(8,128)(2,1)} %w_in_hbm.1, f32[1,48]{1,0:T(1,128)} %bitcast.8, bf16[96,864]{1,0:T(8,128)(2,1)} %w_ent_hbm.1, s32[1,12]{1,0:T(1,128)} %bitcast.9, s32[1,1,1]{2,1,0:T(1,128)S(6)} %copy.11.count_hbm, ...), custom_call_target="tpu_custom_call" | custom-call | flops 1700000000 | bytes 1500000 | tf_op jit(solution)/shard_map/coding_window/pallas_call | solution.py:470
  52.5 0.7 %copy.12 = bf16[1,1,1,12,48,256]{5,4,3,2,1,0:T(8,128)(2,1)} copy(bf16[1,1,1,12,48,256]{5,4,3,2,1,0:T(8,128)(2,1)S(1)} %bitcast.5) | data formatting | bytes 589824
  53.2 0.6 %copy.13 = f32[24,864]{1,0:T(8,128)} copy(f32[24,864]{1,0:T(8,128)S(1)} %get-tuple-element.9) | data formatting | bytes 165888
